TPU v7x, 32 devices: a whole 2x2x4 slice. The times are simulated.
32 devices in a mesh: ctx: 16 (over z, y, core), head: 2 (over x).
Axes of the slice: x: 2, y: 2, z: 4, core: 2. Of those that a mesh axis runs over, the one named last changes fastest.
Arguments:
- hidden_states: bfloat16 [8192, 5376], P('ctx', 'head'), may hold values from -6 to 6
- query_base: bfloat16 [8192, 4096], P('ctx', 'head'), may hold values from -8 to 8
- key_base: bfloat16 [8192, 2048], P('ctx', 'head'), may hold values from -8 to 8
- frozen_value_rows: bfloat16 [8192, 2048], P('ctx', 'head'), may hold values from -6 to 6
- query_down: bfloat16 [5376, 16], P('head'), may hold values from -0.078125 to 0.078125
- query_up: bfloat16 [16, 4096], P(None, 'head'), may hold values from -0.75 to 0.75
- value_down: bfloat16 [5376, 16], P('head'), may hold values from -0.078125 to 0.078125
- value_up_weight: bfloat16 [16, 2048], P(None, 'head'), may hold values from -0.75 to 0.75
- positions: int32 [8192], P('ctx'), may hold values from 0 to 16382, as said below
- block_mask: int32 [64, 9], replicated, may hold values from 0 to 1, as said below
- output_gradient: bfloat16 [8192, 4096], P('ctx', 'head'), may hold values from -96 to 96
Outputs:
- attention_out: bfloat16 [8192, 4096], P('ctx', 'head')
- grad_query_down: float32 [5376, 16], P('head')
- grad_query_up: float32 [16, 4096], P(None, 'head')
- grad_value_down: float32 [5376, 16], P('head')
- grad_value_up: float32 [16, 2048], P(None, 'head')
Inputs may be any that keep to these rules, and one draw needn't show every extreme that they name: positions rise strictly along the tokens. `block_mask`: entry (b, o) is 1 where the query block b may attend the key block b - o; column 0 is 1 in every row.
All inputs are finite; a program needn't handle non-finite values.
Results may differ from a plain program's by a relative error of at most 0.04.
Values may be sent and summed in bfloat16 or wider, within the bound.
No kernel may reach another device: no remote copies, remote signals or barrier semaphores. Data moves between devices by JAX's collectives and lax.ppermute only.
A program may use at most 192 MiB of HBM per device.

v0:
```python
import jax
import jax.numpy as jnp
from jax import lax
from jax.sharding import PartitionSpec as P

D = 5376
QUERY_HEADS = 32
KEY_VALUE_HEADS = 16
HEAD_SIZE = 128
WINDOW = 1024
BLOCK = 128


rope_base = 10000.0


def shifted(x, axis, by):
    devices = lax.axis_size(axis)
    pairs = [(i, i + by) for i in range(devices) if 0 <= i + by < devices]
    return lax.ppermute(x, axis, pairs)


def rotate(row_block, position_ids, turn_sign):
    count = row_block.shape[0]
    col_count = row_block.shape[1]
    half_width = HEAD_SIZE // 2
    frequency = rope_base ** (-(2.0 * jnp.arange(half_width, dtype=jnp.float32)) / HEAD_SIZE)
    angles = position_ids.astype(jnp.float32)[:, None] * frequency[None, :]
    cosines = jnp.concatenate([jnp.cos(angles), jnp.cos(angles)], axis=-1)
    sines = jnp.concatenate([jnp.sin(angles), jnp.sin(angles)], axis=-1)
    shaped = row_block.reshape(count, col_count // HEAD_SIZE, HEAD_SIZE)
    turned = jnp.concatenate([-shaped[..., half_width:], shaped[..., :half_width]], axis=-1)
    return (shaped * cosines[:, None, :] + turn_sign * turned * sines[:, None, :]).reshape(
        count, col_count
    )


def allowed_pairs(mask_rows, query_first, key_first, count_of_queries, key_count):
    query_ids = query_first + jnp.arange(count_of_queries, dtype=jnp.int32)
    key_ids = key_first + jnp.arange(key_count, dtype=jnp.int32)
    token_gap = key_ids[None, :] - query_ids[:, None]
    token_ok = (token_gap <= 0) & (token_gap > -WINDOW) & (key_ids >= 0)[None, :]
    query_blocks = query_first // BLOCK + jnp.arange(count_of_queries // BLOCK, dtype=jnp.int32)
    key_blocks = key_first // BLOCK + jnp.arange(key_count // BLOCK, dtype=jnp.int32)
    offset = query_blocks[:, None] - key_blocks[None, :]
    band_size = mask_rows.shape[1]
    band_hit = jnp.any(
        (offset[:, :, None] == jnp.arange(band_size, dtype=jnp.int32)[None, None, :])
        & (mask_rows[:, None, :] == 1),
        axis=-1,
    )
    spread_out = jnp.broadcast_to(
        band_hit[:, None, :, None], (count_of_queries // BLOCK, BLOCK, key_count // BLOCK, BLOCK)
    ).reshape(count_of_queries, key_count)
    return token_ok & spread_out


def head_scores(query_rows, key_rows, head_index, score_scale):
    count_of_queries = query_rows.shape[0]
    query_groups = QUERY_HEADS // KEY_VALUE_HEADS
    head_queries = lax.dynamic_slice_in_dim(
        query_rows, head_index * query_groups * HEAD_SIZE, query_groups * HEAD_SIZE, 1
    ).reshape(count_of_queries, query_groups, HEAD_SIZE)
    head_keys = lax.dynamic_slice_in_dim(key_rows, head_index * HEAD_SIZE, HEAD_SIZE, 1)
    return (
        jnp.einsum("lgd,kd->glk", head_queries, head_keys, preferred_element_type=jnp.float32)
        * score_scale,
        head_keys,
    )


def attend(query_rows, key_rows, value_rows, allowed, score_scale):
    count_of_queries = query_rows.shape[0]
    kv_heads = key_rows.shape[1] // HEAD_SIZE
    query_groups = QUERY_HEADS // KEY_VALUE_HEADS
    group_width = query_groups * HEAD_SIZE

    def attend_one_head(head_index, loop_state):
        attn_out, log_totals = loop_state
        scores, head_keys = head_scores(query_rows, key_rows, head_index, score_scale)
        scores = jnp.where(allowed[None], scores, -jnp.inf)
        row_max = jnp.max(scores, axis=-1, keepdims=True)
        log_total = row_max[..., 0] + jnp.log(jnp.sum(jnp.exp(scores - row_max), axis=-1))
        rounded_length = jnp.exp(scores - log_total[..., None]).astype(jnp.bfloat16)
        head_values = lax.dynamic_slice_in_dim(value_rows, head_index * HEAD_SIZE, HEAD_SIZE, 1)
        head_out = jnp.einsum(
            "glk,kd->lgd", rounded_length, head_values, preferred_element_type=jnp.float32
        ).astype(jnp.bfloat16)
        attn_out = lax.dynamic_update_slice_in_dim(
            attn_out, head_out.reshape(count_of_queries, group_width), head_index * group_width, 1
        )
        log_totals = lax.dynamic_update_slice_in_dim(log_totals, log_total[None], head_index, 0)
        return (attn_out, log_totals)

    initial = (
        jnp.zeros((count_of_queries, kv_heads * group_width), jnp.bfloat16),
        jnp.zeros((kv_heads, query_groups, count_of_queries), jnp.float32),
    )
    return lax.fori_loop(0, kv_heads, attend_one_head, initial)


def backward(
    query_rows,
    key_rows,
    value_rows,
    allowed,
    log_totals,
    output_gradient,
    attention_out,
    score_scale,
):
    count_of_queries = query_rows.shape[0]
    key_count = key_rows.shape[0]
    kv_heads = key_rows.shape[1] // HEAD_SIZE
    query_groups = QUERY_HEADS // KEY_VALUE_HEADS
    group_width = query_groups * HEAD_SIZE

    def backward_one_head(head_index, loop_state):
        query_sums, value_sums = loop_state
        scores, head_keys = head_scores(query_rows, key_rows, head_index, score_scale)
        log_total = lax.dynamic_index_in_dim(log_totals, head_index, 0, keepdims=False)
        weights = jnp.exp(jnp.where(allowed[None], scores, -jnp.inf) - log_total[..., None])
        rounded_length = weights.astype(jnp.bfloat16)
        head_values = lax.dynamic_slice_in_dim(value_rows, head_index * HEAD_SIZE, HEAD_SIZE, 1)
        head_grads = lax.dynamic_slice_in_dim(
            output_gradient, head_index * group_width, group_width, 1
        ).reshape(count_of_queries, query_groups, HEAD_SIZE)
        head_outs = lax.dynamic_slice_in_dim(
            attention_out, head_index * group_width, group_width, 1
        ).reshape(count_of_queries, query_groups, HEAD_SIZE)
        row_delta = jnp.sum(head_grads.astype(jnp.float32) * head_outs.astype(jnp.float32), axis=-1)
        grad_weights = jnp.einsum(
            "lgd,kd->glk", head_grads, head_values, preferred_element_type=jnp.float32
        )
        grad_scores = (weights * (grad_weights - row_delta.T[:, :, None]) * score_scale).astype(
            jnp.bfloat16
        )
        query_part = jnp.einsum(
            "glk,kd->lgd", grad_scores, head_keys, preferred_element_type=jnp.float32
        ).reshape(count_of_queries, group_width)
        value_portion = jnp.einsum(
            "glk,lgd->kd", rounded_length, head_grads, preferred_element_type=jnp.float32
        )
        query_sums = lax.dynamic_update_slice_in_dim(
            query_sums, query_part, head_index * group_width, 1
        )
        value_sums = lax.dynamic_update_slice_in_dim(
            value_sums, value_portion, head_index * HEAD_SIZE, 1
        )
        return (query_sums, value_sums)

    initial = (
        jnp.zeros((count_of_queries, kv_heads * group_width), jnp.float32),
        jnp.zeros((key_count, kv_heads * HEAD_SIZE), jnp.float32),
    )
    return lax.fori_loop(0, kv_heads, backward_one_head, initial)


def per_device(
    hidden_states,
    query_base,
    key_base,
    frozen_value_rows,
    query_down,
    query_up,
    value_down,
    value_up_weight,
    positions,
    block_mask,
    output_gradient,
):
    count_of_queries = hidden_states.shape[0]
    key_extent = WINDOW // count_of_queries
    key_range_length = (key_extent + 1) * count_of_queries
    score_scale = (D // QUERY_HEADS) ** (-0.5)
    mask_height = count_of_queries // BLOCK
    device_index = lax.axis_index("ctx")
    leading_token = device_index * count_of_queries
    tokens_all = count_of_queries * lax.axis_size("ctx")
    query_sum, value_sum = lax.psum(
        (
            jnp.dot(hidden_states, query_down, preferred_element_type=jnp.float32),
            jnp.dot(hidden_states, value_down, preferred_element_type=jnp.float32),
        ),
        "head",
    )
    query_low = query_sum.astype(jnp.bfloat16)
    value_low = value_sum.astype(jnp.bfloat16)
    query_rows = rotate(
        query_base.astype(jnp.float32)
        + jnp.dot(query_low, query_up, preferred_element_type=jnp.float32),
        positions,
        1.0,
    ).astype(jnp.bfloat16)
    key_rows = rotate(key_base.astype(jnp.float32), positions, 1.0).astype(jnp.bfloat16)
    values = (
        frozen_value_rows.astype(jnp.float32)
        + jnp.dot(value_low, value_up_weight, preferred_element_type=jnp.float32)
    ).astype(jnp.bfloat16)
    earlier = []
    for distance in range(key_extent, 0, -1):
        earlier.append(shifted((key_rows, values), "ctx", distance))
    window_key_rows = jnp.concatenate([pair[0] for pair in earlier] + [key_rows], axis=0)
    window_value_rows = jnp.concatenate([pair[1] for pair in earlier] + [values], axis=0)
    own_mask = lax.dynamic_slice_in_dim(block_mask, device_index * mask_height, mask_height, 0)
    allowed = allowed_pairs(
        own_mask,
        leading_token,
        leading_token - key_extent * count_of_queries,
        count_of_queries,
        key_range_length,
    )
    attention_out, log_totals = attend(
        query_rows, window_key_rows, window_value_rows, allowed, score_scale
    )
    query_sums, value_sums = backward(
        query_rows,
        window_key_rows,
        window_value_rows,
        allowed,
        log_totals,
        output_gradient,
        attention_out,
        score_scale,
    )
    value_total = value_sums[key_extent * count_of_queries :]
    for distance in range(1, key_extent + 1):
        partial_value = value_sums[
            (key_extent - distance)
            * count_of_queries : (key_extent - distance + 1)
            * count_of_queries
        ]
        value_total = value_total + shifted(partial_value, "ctx", -distance)
    query_grad = rotate(query_sums, positions, -1.0).astype(jnp.bfloat16)
    value_grad = value_total.astype(jnp.bfloat16)
    contract_cols = (((1,), (1,)), ((), ()))
    contract_rows = (((0,), (0,)), ((), ()))
    query_part = lax.dot_general(
        query_grad, query_up, contract_cols, preferred_element_type=jnp.float32
    )
    value_portion = lax.dot_general(
        value_grad, value_up_weight, contract_cols, preferred_element_type=jnp.float32
    )
    query_back_sum, value_back_sum = lax.psum((query_part, value_portion), "head")
    query_back = query_back_sum.astype(jnp.bfloat16)
    value_back = value_back_sum.astype(jnp.bfloat16)
    down_query = lax.dot_general(
        hidden_states, query_back, contract_rows, preferred_element_type=jnp.float32
    )
    down_value = lax.dot_general(
        hidden_states, value_back, contract_rows, preferred_element_type=jnp.float32
    )
    up_query = lax.dot_general(
        query_low, query_grad, contract_rows, preferred_element_type=jnp.float32
    )
    up_value = lax.dot_general(
        value_low, value_grad, contract_rows, preferred_element_type=jnp.float32
    )
    summed = lax.psum((down_query, up_query, down_value, up_value), "ctx")
    loss_scale = tokens_all ** (-0.5)
    return (
        attention_out,
        summed[0] * loss_scale,
        summed[1] * loss_scale,
        summed[2] * loss_scale,
        summed[3] * loss_scale,
    )


def solution(mesh):
    placed = (
        P("ctx", "head"),
        P("ctx", "head"),
        P("ctx", "head"),
        P("ctx", "head"),
        P("head", None),
        P(None, "head"),
        P("head", None),
        P(None, "head"),
        P("ctx"),
        P(),
        P("ctx", "head"),
    )
    return jax.shard_map(
        per_device,
        mesh=mesh,
        in_specs=placed,
        out_specs=(
            P("ctx", "head"),
            P("head", None),
            P(None, "head"),
            P("head", None),
            P(None, "head"),
        ),
        check_vma=False,
    )
```

profile of v0, /device:TPU:0, one launch (start us, length us, event | category | flops | bytes accessed | tf_op | source)
XLA Modules:
  0.0 586.5 jit_solution(9332172508343341022)
XLA Ops:
  15.7 6.1 %collective-permute-start.2 = (bf16[512,1024]{1,0:T(8,128)(2,1)}, bf16[512,1024]{1,0:T(8,128)(2,1)}, u32[]{:S(2)}, u32[]{:S(2)}) collective-permute-start(bf16[512,1024]{1,0:T(8,128)(2,1)} %fusion.59), channel_id=1, source_target_pairs={{0,4},{2,6},{4,8},{6,10},{8,12},{10,14},{12,16},{14,18},{16,20},{1... | collective-permute-start | bytes 3145736 | tf_op jit(solution)/shard_map/ppermute | solution.py:20
  25.9 8.9 %all-reduce.2 = (bf16[512,16]{0,1:T(8,128)(2,1)S(1)}, bf16[512,16]{0,1:T(8,128)(2,1)S(1)}) all-reduce(f32[512,16]{0,1:T(8,128)S(1)} %fusion.72, f32[512,16]{0,1:T(8,128)S(1)} %fusion.73), channel_id=1, replica_groups=mesh['ctx'=16,'head'=2] {'head'}, use_global_device_ids=true, to_apply=%region_2.3 | all-reduce | flops 16384 | bytes 98304 | tf_op jit(solution)/shard_map/psum | solution.py:180
  71.7 95.8 %while.36 = (s32[]{:T(128)}, bf16[512,2048]{0,1:T(8,128)(2,1)}, f32[8,2,512]{2,1,0:T(2,128)}, bf16[1536,1024]{1,0:T(8,128)(2,1)}, bf16[1536,1024]{1,0:T(8,128)(2...) while((s32[]{:T(128)}, bf16[512,2048]{0,1:T(8,128)(2,1)}, ...), condition=%wide.region_6.7_spmd.clone, body=%wide.region_3.6_spmd.clone.sunk | while | flops 827456512 | bytes 25995568 | solution.py:99
  173.4 192.9 %while.37 = (s32[]{:T(128)}, f32[512,2048]{0,1:T(8,128)}, f32[1536,1024]{1,0:T(8,128)}, bf16[1536,1024]{1,0:T(8,128)(2,1)}, bf16[512,2048]{0,1:T(8,128)(2,1)}, /...) while((s32[]{:T(128)}, f32[512,2048]{0,1:T(8,128)}, ...), condition=%wide.region_9.10_spmd.clone, body=%wide.region_7.9_spmd.clone.sunk | while | flops 1633156096 | bytes 32426892 | solution.py:156
  174.6 4.6 fusion.131
  183.9 5.2 fusion.135
  190.8 6.0 %fusion.134 = f32[128,2,512]{2,0,1:T(8,128)S(1)} fusion(f32[1536,512,2]{1,0,2:T(8,128)} %fusion.131, bf16[512,2,128]{0,2,1:T(8,128)(2,1)S(1)} %bitcast.218, f32[2,512]{1,0:T(2,128)} %bitcast.227, f32[2,512]{1,0:T(2,128)} %copy-done.12, pred[512,1536]{0,1:T(8,128)(4,1)} %copy-done.3, bf16[1536,1024]{1,0:T(8,128)(2,1)} %get-tuple-element.882, ...), kind=kOutput, calls=%fused_computation.44.clone.1 | convolution fusion | flops 816316416 | bytes 8659968 | tf_op jit(solution)/shard_map/while/body/eval_jaxpr/glk,kd->lgd/dot_general | solution.py:138
  208.0 5.2 fusion.135
  214.9 6.0 %fusion.134 = f32[128,2,512]{2,0,1:T(8,128)S(1)} fusion(f32[1536,512,2]{1,0,2:T(8,128)} %fusion.131, bf16[512,2,128]{0,2,1:T(8,128)(2,1)S(1)} %bitcast.218, f32[2,512]{1,0:T(2,128)} %bitcast.227, f32[2,512]{1,0:T(2,128)} %copy-done.12, pred[512,1536]{0,1:T(8,128)(4,1)} %copy-done.3, bf16[1536,1024]{1,0:T(8,128)(2,1)} %get-tuple-element.882, ...), kind=kOutput, calls=%fused_computation.44.clone.1 | convolution fusion | flops 816316416 | bytes 8659968 | tf_op jit(solution)/shard_map/while/body/eval_jaxpr/glk,kd->lgd/dot_general | solution.py:138
  232.0 5.3 fusion.135
  239.0 6.0 %fusion.134 = f32[128,2,512]{2,0,1:T(8,128)S(1)} fusion(f32[1536,512,2]{1,0,2:T(8,128)} %fusion.131, bf16[512,2,128]{0,2,1:T(8,128)(2,1)S(1)} %bitcast.218, f32[2,512]{1,0:T(2,128)} %bitcast.227, f32[2,512]{1,0:T(2,128)} %copy-done.12, pred[512,1536]{0,1:T(8,128)(4,1)} %copy-done.3, bf16[1536,1024]{1,0:T(8,128)(2,1)} %get-tuple-element.882, ...), kind=kOutput, calls=%fused_computation.44.clone.1 | convolution fusion | flops 816316416 | bytes 8659968 | tf_op jit(solution)/shard_map/while/body/eval_jaxpr/glk,kd->lgd/dot_general | solution.py:138
  246.8 4.6 fusion.131
  256.1 5.2 fusion.135
  263.0 6.1 %fusion.134 = f32[128,2,512]{2,0,1:T(8,128)S(1)} fusion(f32[1536,512,2]{1,0,2:T(8,128)} %fusion.131, bf16[512,2,128]{0,2,1:T(8,128)(2,1)S(1)} %bitcast.218, f32[2,512]{1,0:T(2,128)} %bitcast.227, f32[2,512]{1,0:T(2,128)} %copy-done.12, pred[512,1536]{0,1:T(8,128)(4,1)} %copy-done.3, bf16[1536,1024]{1,0:T(8,128)(2,1)} %get-tuple-element.882, ...), kind=kOutput, calls=%fused_computation.44.clone.1 | convolution fusion | flops 816316416 | bytes 8659968 | tf_op jit(solution)/shard_map/while/body/eval_jaxpr/glk,kd->lgd/dot_general | solution.py:138
  270.9 4.6 fusion.131
  280.3 5.3 fusion.135
  287.1 6.0 %fusion.134 = f32[128,2,512]{2,0,1:T(8,128)S(1)} fusion(f32[1536,512,2]{1,0,2:T(8,128)} %fusion.131, bf16[512,2,128]{0,2,1:T(8,128)(2,1)S(1)} %bitcast.218, f32[2,512]{1,0:T(2,128)} %bitcast.227, f32[2,512]{1,0:T(2,128)} %copy-done.12, pred[512,1536]{0,1:T(8,128)(4,1)} %copy-done.3, bf16[1536,1024]{1,0:T(8,128)(2,1)} %get-tuple-element.882, ...), kind=kOutput, calls=%fused_computation.44.clone.1 | convolution fusion | flops 816316416 | bytes 8659968 | tf_op jit(solution)/shard_map/while/body/eval_jaxpr/glk,kd->lgd/dot_general | solution.py:138
  304.3 5.2 fusion.135
  311.2 6.0 %fusion.134 = f32[128,2,512]{2,0,1:T(8,128)S(1)} fusion(f32[1536,512,2]{1,0,2:T(8,128)} %fusion.131, bf16[512,2,128]{0,2,1:T(8,128)(2,1)S(1)} %bitcast.218, f32[2,512]{1,0:T(2,128)} %bitcast.227, f32[2,512]{1,0:T(2,128)} %copy-done.12, pred[512,1536]{0,1:T(8,128)(4,1)} %copy-done.3, bf16[1536,1024]{1,0:T(8,128)(2,1)} %get-tuple-element.882, ...), kind=kOutput, calls=%fused_computation.44.clone.1 | convolution fusion | flops 816316416 | bytes 8659968 | tf_op jit(solution)/shard_map/while/body/eval_jaxpr/glk,kd->lgd/dot_general | solution.py:138
  328.3 5.2 fusion.135
  335.2 6.0 %fusion.134 = f32[128,2,512]{2,0,1:T(8,128)S(1)} fusion(f32[1536,512,2]{1,0,2:T(8,128)} %fusion.131, bf16[512,2,128]{0,2,1:T(8,128)(2,1)S(1)} %bitcast.218, f32[2,512]{1,0:T(2,128)} %bitcast.227, f32[2,512]{1,0:T(2,128)} %copy-done.12, pred[512,1536]{0,1:T(8,128)(4,1)} %copy-done.3, bf16[1536,1024]{1,0:T(8,128)(2,1)} %get-tuple-element.882, ...), kind=kOutput, calls=%fused_computation.44.clone.1 | convolution fusion | flops 816316416 | bytes 8659968 | tf_op jit(solution)/shard_map/while/body/eval_jaxpr/glk,kd->lgd/dot_general | solution.py:138
  352.4 5.3 fusion.135
  359.3 6.2 %fusion.134 = f32[128,2,512]{2,0,1:T(8,128)S(1)} fusion(f32[1536,512,2]{1,0,2:T(8,128)} %fusion.131, bf16[512,2,128]{0,2,1:T(8,128)(2,1)S(1)} %bitcast.218, f32[2,512]{1,0:T(2,128)} %bitcast.227, f32[2,512]{1,0:T(2,128)} %copy-done.12, pred[512,1536]{0,1:T(8,128)(4,1)} %copy-done.3, bf16[1536,1024]{1,0:T(8,128)(2,1)} %get-tuple-element.882, ...), kind=kOutput, calls=%fused_computation.44.clone.1 | convolution fusion | flops 816316416 | bytes 8659968 | tf_op jit(solution)/shard_map/while/body/eval_jaxpr/glk,kd->lgd/dot_general | solution.py:138
  366.3 4.9 fusion.70
  373.8 5.7 copy.54
  379.5 4.9 fusion.71
  384.4 4.9 copy.68
  393.7 4.9 copy.69
  398.6 4.7 maximum_multiply_fusion.1
  410.8 55.3 %collective-permute-done.5 = f32[512,1024]{1,0:T(8,128)} collective-permute-done((f32[512,1024]{1,0:T(8,128)}, f32[512,1024]{1,0:T(8,128)}, u32[]{:S(2)}, u32[]{:S(2)}) %collective-permute-start.5) | collective-permute-done | bytes 2097184 | tf_op jit(solution)/shard_map/ppermute | solution.py:20
  470.8 8.9 %all-reduce.1 = (bf16[512,16]{0,1:T(8,128)(2,1)S(1)}, bf16[512,16]{0,1:T(8,128)(2,1)S(1)}) all-reduce(f32[512,16]{0,1:T(8,128)S(1)} %fusion.74, f32[512,16]{0,1:T(8,128)S(1)} %fusion.75), channel_id=1, replica_groups=mesh['ctx'=16,'head'=2] {'head'}, use_global_device_ids=true, to_apply=%region_10.11 | all-reduce | flops 16384 | bytes 98304 | tf_op jit(solution)/shard_map/psum | solution.py:244
  486.0 87.2 %all-reduce.5.cloned.1.call-done = (f32[2688,16]{0,1:T(8,128)}, f32[16,2048]{1,0:T(8,128)}, f32[2688,16]{0,1:T(8,128)}, f32[16,1024]{1,0:T(8,128)}) async-done(((f32[2688,16]{0,1:T(8,128)}, f32[16,2048]{1,0:T(8,128)}, f32[2688,16]{0,1:T(8,128)}, f32[16,1024]{1,0:T(8,128)}), (f32[2688,16]{0,1:T(8,128)}, f32[16,2048]{1,0:T(8,128)}, f32[2688,16]{0,1:T(8,128)}, ...) | async-done | bytes 540688 | tf_op jit(solution)/shard_map/psum | solution.py:259
  (262 shorter events, 270.5 us)
Async XLA Ops:
  7.2 17.1 %copy-start = (bf16[512,2688]{1,0:T(8,128)(2,1)S(1)}, bf16[512,2688]{1,0:T(8,128)(2,1)}, u32[]{:S(2)}) copy-start(bf16[512,2688]{1,0:T(8,128)(2,1)} %param.15) | copy-start | bytes 8257540
  7.2 566.0 %all-reduce.5.cloned.1.call-start = ((), (), s32[]{:S(2)}) async-start(), calls=%async_computation | async-start | bytes 1081344 | tf_op jit(solution)/shard_map/psum | solution.py:259
  13.8 10.4 %copy-start.13 = (bf16[2688,16]{0,1:T(8,128)(2,1)S(1)}, bf16[2688,16]{0,1:T(8,128)(2,1)}, u32[]{:S(2)}) copy-start(bf16[2688,16]{0,1:T(8,128)(2,1)} %param.21) | copy-start | bytes 258052
  15.7 9.4 %copy-start.14 = (bf16[2688,16]{0,1:T(8,128)(2,1)S(1)}, bf16[2688,16]{0,1:T(8,128)(2,1)}, u32[]{:S(2)}) copy-start(bf16[2688,16]{0,1:T(8,128)(2,1)} %param.19) | copy-start | bytes 258052
  15.7 46.2 %collective-permute-start.2 = (bf16[512,1024]{1,0:T(8,128)(2,1)}, bf16[512,1024]{1,0:T(8,128)(2,1)}, u32[]{:S(2)}, u32[]{:S(2)}) collective-permute-start(bf16[512,1024]{1,0:T(8,128)(2,1)} %fusion.59), channel_id=1, source_target_pairs={{0,4},{2,6},{4,8},{6,10},{8,12},{10,14},{12,16},{14,18},{16,20},{1... | collective-permute-start | bytes 3145736 | tf_op jit(solution)/shard_map/ppermute | solution.py:20
  21.7 40.2 %collective-permute-start.3 = (bf16[512,1024]{1,0:T(8,128)(2,1)}, bf16[512,1024]{1,0:T(8,128)(2,1)}, u32[]{:S(2)}, u32[]{:S(2)}) collective-permute-start(bf16[512,1024]{1,0:T(8,128)(2,1)} %fusion.59), channel_id=1, source_target_pairs={{0,2},{2,4},{4,6},{6,8},{8,10},{10,12},{12,14},{14,16},{16,18},{18... | collective-permute-start | bytes 3145736 | tf_op jit(solution)/shard_map/ppermute | solution.py:20
  25.1 9.8 %copy-start.10 = (bf16[16,1024]{1,0:T(8,128)(2,1)S(1)}, bf16[16,1024]{1,0:T(8,128)(2,1)}, u32[]{:S(2)}) copy-start(bf16[16,1024]{1,0:T(8,128)(2,1)} %param.22) | copy-start | bytes 98308
  25.1 19.1 %copy-start.8 = (bf16[16,2048]{1,0:T(8,128)(2,1)S(1)}, bf16[16,2048]{1,0:T(8,128)(2,1)}, u32[]{:S(2)}) copy-start(bf16[16,2048]{1,0:T(8,128)(2,1)} %param.20) | copy-start | bytes 196612
  34.8 10.1 %copy-start.15 = (bf16[512,16]{0,1:T(8,128)(2,1)}, bf16[512,16]{0,1:T(8,128)(2,1)S(1)}, u32[]{:S(2)}) copy-start(bf16[512,16]{0,1:T(8,128)(2,1)S(1)} %get-tuple-element.623) | copy-start | bytes 49156
  34.8 10.1 %copy-start.17 = (bf16[512,16]{0,1:T(8,128)(2,1)}, bf16[512,16]{0,1:T(8,128)(2,1)S(1)}, u32[]{:S(2)}) copy-start(bf16[512,16]{0,1:T(8,128)(2,1)S(1)} %get-tuple-element.624) | copy-start | bytes 49156
  34.8 9.3 %copy-start.6 = (bf16[512,2048]{1,0:T(8,128)(2,1)S(1)}, bf16[512,2048]{1,0:T(8,128)(2,1)}, u32[]{:S(2)}) copy-start(bf16[512,2048]{1,0:T(8,128)(2,1)} %param.16) | copy-start | bytes 6291460
  37.7 29.4 %collective-permute-start = (bf16[512,1024]{1,0:T(8,128)(2,1)}, bf16[512,1024]{1,0:T(8,128)(2,1)}, u32[]{:S(2)}, u32[]{:S(2)}) collective-permute-start(bf16[512,1024]{1,0:T(8,128)(2,1)} %add_convert_fusion.1), channel_id=1, source_target_pairs={{0,4},{2,6},{4,8},{6,10},{8,12},{10,14},{12,16},{14,18},{16,20},{1... | collective-permute-start | bytes 3145736 | tf_op jit(solution)/shard_map/ppermute | solution.py:20
  40.6 26.4 %collective-permute-start.1 = (bf16[512,1024]{1,0:T(8,128)(2,1)}, bf16[512,1024]{1,0:T(8,128)(2,1)}, u32[]{:S(2)}, u32[]{:S(2)}) collective-permute-start(bf16[512,1024]{1,0:T(8,128)(2,1)} %add_convert_fusion.1), channel_id=1, source_target_pairs={{0,2},{2,4},{4,6},{6,8},{8,10},{10,12},{12,14},{14,16},{16,18},{18... | collective-permute-start | bytes 3145736 | tf_op jit(solution)/shard_map/ppermute | solution.py:20
  183.2 6.0 %copy-start.3 = (pred[512,1536]{0,1:T(8,128)(4,1)}, pred[512,1536]{0,1:T(8,128)(4,1)S(1)}, u32[]{:S(2)}) copy-start(pred[512,1536]{0,1:T(8,128)(4,1)S(1)} %fusion.133) | copy-start | bytes 2359300 | tf_op jit(solution)/shard_map/while
  183.9 5.3 copy-start.12
  207.3 6.0 %copy-start.3 = (pred[512,1536]{0,1:T(8,128)(4,1)}, pred[512,1536]{0,1:T(8,128)(4,1)S(1)}, u32[]{:S(2)}) copy-start(pred[512,1536]{0,1:T(8,128)(4,1)S(1)} %fusion.133) | copy-start | bytes 2359300 | tf_op jit(solution)/shard_map/while
  208.0 5.3 copy-start.12
  231.3 6.0 %copy-start.3 = (pred[512,1536]{0,1:T(8,128)(4,1)}, pred[512,1536]{0,1:T(8,128)(4,1)S(1)}, u32[]{:S(2)}) copy-start(pred[512,1536]{0,1:T(8,128)(4,1)S(1)} %fusion.133) | copy-start | bytes 2359300 | tf_op jit(solution)/shard_map/while
  232.0 5.3 copy-start.12
  255.4 6.0 %copy-start.3 = (pred[512,1536]{0,1:T(8,128)(4,1)}, pred[512,1536]{0,1:T(8,128)(4,1)S(1)}, u32[]{:S(2)}) copy-start(pred[512,1536]{0,1:T(8,128)(4,1)S(1)} %fusion.133) | copy-start | bytes 2359300 | tf_op jit(solution)/shard_map/while
  279.5 6.0 %copy-start.3 = (pred[512,1536]{0,1:T(8,128)(4,1)}, pred[512,1536]{0,1:T(8,128)(4,1)S(1)}, u32[]{:S(2)}) copy-start(pred[512,1536]{0,1:T(8,128)(4,1)S(1)} %fusion.133) | copy-start | bytes 2359300 | tf_op jit(solution)/shard_map/while
  280.3 5.3 copy-start.12
  303.6 6.0 %copy-start.3 = (pred[512,1536]{0,1:T(8,128)(4,1)}, pred[512,1536]{0,1:T(8,128)(4,1)S(1)}, u32[]{:S(2)}) copy-start(pred[512,1536]{0,1:T(8,128)(4,1)S(1)} %fusion.133) | copy-start | bytes 2359300 | tf_op jit(solution)/shard_map/while
  304.3 5.3 copy-start.12
  327.6 6.0 %copy-start.3 = (pred[512,1536]{0,1:T(8,128)(4,1)}, pred[512,1536]{0,1:T(8,128)(4,1)S(1)}, u32[]{:S(2)}) copy-start(pred[512,1536]{0,1:T(8,128)(4,1)S(1)} %fusion.133) | copy-start | bytes 2359300 | tf_op jit(solution)/shard_map/while
  351.6 6.0 %copy-start.3 = (pred[512,1536]{0,1:T(8,128)(4,1)}, pred[512,1536]{0,1:T(8,128)(4,1)S(1)}, u32[]{:S(2)}) copy-start(pred[512,1536]{0,1:T(8,128)(4,1)S(1)} %fusion.133) | copy-start | bytes 2359300 | tf_op jit(solution)/shard_map/while
  352.4 5.3 copy-start.12
  371.2 39.6 %collective-permute-start.4 = (f32[512,1024]{1,0:T(8,128)}, f32[512,1024]{1,0:T(8,128)}, u32[]{:S(2)}, u32[]{:S(2)}) collective-permute-start(f32[512,1024]{1,0:T(8,128)} %get-tuple-element.629), channel_id=1, source_target_pairs={{2,0},{4,2},{6,4},{8,6},{10,8},{12,10},{14,12},{16,14},{18,16},{20... | collective-permute-start | bytes 6291464 | tf_op jit(solution)/shard_map/ppermute | solution.py:20
  372.5 93.7 %collective-permute-start.5 = (f32[512,1024]{1,0:T(8,128)}, f32[512,1024]{1,0:T(8,128)}, u32[]{:S(2)}, u32[]{:S(2)}) collective-permute-start(f32[512,1024]{1,0:T(8,128)} %get-tuple-element.630), channel_id=1, source_target_pairs={{4,0},{6,2},{8,4},{10,6},{12,8},{14,10},{16,12},{18,14},{20,16},{2... | collective-permute-start | bytes 6291464 | tf_op jit(solution)/shard_map/ppermute | solution.py:20
  398.6 5.9 %copy-start.4 = (f32[512,2048]{1,0:T(8,128)S(1)}, f32[512,2048]{1,0:T(8,128)}, u32[]{:S(2)}) copy-start(f32[512,2048]{1,0:T(8,128)} %copy.54) | copy-start | bytes 12582916
  410.8 58.8 %copy-start.11 = (bf16[16,1024]{1,0:T(8,128)(2,1)S(1)}, bf16[16,1024]{1,0:T(8,128)(2,1)}, u32[]{:S(2)}) copy-start(bf16[16,1024]{1,0:T(8,128)(2,1)} %param.22) | copy-start | bytes 98308
  410.8 59.1 %copy-start.16 = (bf16[512,16]{0,1:T(8,128)(2,1)S(1)}, bf16[512,16]{0,1:T(8,128)(2,1)}, u32[]{:S(2)}) copy-start(bf16[512,16]{0,1:T(8,128)(2,1)} %copy-done.15) | copy-start | bytes 49156
  (9 other events, 38.9 us)
Sparse Core Ops, SparseCore 0:
  482.2 90.9 all-reduce.4
where the time goes:
time: 595 us; the launch traced here: 587 us
  matrix products  180 us (30%)
  waiting for transfers between devices  144 us (24%)
  other arithmetic  117 us (20%)
  local copies, waits for them, and re-layouts  94.5 us (16%)
  blocking collectives  17.8 us (3%)
  starting transfers between devices  17.6 us (3%)
  between operations  14.6 us (2%)
    psum x1, waiting for transfers between devices, per_device(): summed = lax.psum((down_query, up_query, down_value, up_value), 'ctx')  87.2 us
    ppermute x6, waiting for transfers between devices, shifted(): return lax.ppermute(x, axis, pairs)  57.3 us
    dot_general x16, matrix products, head_scores(): jnp.einsum('lgd,kd->glk', head_queries, head_keys, preferred_element_type...  55.1 us
    dot_general x8, matrix products, backward_one_head(): jnp.einsum('glk,kd->lgd', grad_scores, head_keys, preferred_element_type=...  48.3 us
    dot_general x8, matrix products, backward_one_head(): jnp.einsum('glk,lgd->kd', rounded_length, head_grads, preferred_element_t...  42 us
    and x16, other arithmetic, allowed_pairs(): return token_ok & spread_out  38.9 us
    dot_general x8, matrix products, attend_one_head(): jnp.einsum('glk,kd->lgd', rounded_length, head_values, preferred_element_...  23.7 us
    unnamed x43, local copies, waits for them, and re-layouts  21 us
  transfers between devices with their start and end apart: 7, of which 3 were waited for; matrix products, arithmetic and copies ran while one was open for 11% of the time, Pallas kernels for 0%

commit v1 on v0

v1 whole, which is shorter than its diff:
```python
import functools

import jax
import jax.numpy as jnp
from jax import lax
from jax.experimental import pallas as pl
from jax.experimental.pallas import tpu as pltpu
from jax.sharding import PartitionSpec as P

D = 5376
QUERY_HEADS = 32
KEY_VALUE_HEADS = 16
HEAD_SIZE = 128
WINDOW = 1024
BLOCK = 128
GROUPS = QUERY_HEADS // KEY_VALUE_HEADS
GROUP_WIDTH = GROUPS * HEAD_SIZE
SCORE_SCALE = (D // QUERY_HEADS) ** (-0.5)
LOG2_E = 1.4426950408889634
ROPE_BASE = 10000.0
FORBIDDEN = -1e30
RANK = 16

SUB = 256
KEYS = SUB + WINDOW
LANES = 128

CHUNKS = ((0, 3), (3, 6), (6, 8))

ROWS_BY_COLS = (((1,), (0,)), ((), ()))
BOTH_MINOR = (((1,), (1,)), ((), ()))
BOTH_MAJOR = (((0,), (0,)), ((), ()))


def mm(left, right, dims=ROWS_BY_COLS):
    return lax.dot_general(left, right, dims, preferred_element_type=jnp.float32)


def swap_halves(x):
    return pltpu.roll(x, HEAD_SIZE // 2, 1)


def prologue_kernel(chunks, positions_ref, frequency_ref, key_ref, value_ref, cos_ref, sin_ref, *outs):
    angles = positions_ref[...].astype(jnp.float32) * frequency_ref[...]
    lane = lax.broadcasted_iota(jnp.int32, angles.shape, 1)
    cosines = jnp.cos(angles)
    sines = jnp.sin(angles)
    sines = jnp.where(lane < HEAD_SIZE // 2, -sines, sines)
    cos_ref[...] = cosines
    sin_ref[...] = sines
    for (first, last), out_ref in zip(chunks, outs):
        count = last - first
        for head in range(first, last):
            cols = pl.ds(head * HEAD_SIZE, HEAD_SIZE)
            key = key_ref[:, cols].astype(jnp.float32)
            turned = key * cosines + swap_halves(key) * sines
            out_ref[:, pl.ds((head - first) * HEAD_SIZE, HEAD_SIZE)] = turned.astype(jnp.bfloat16)
            out_ref[:, pl.ds((count + head - first) * HEAD_SIZE, HEAD_SIZE)] = value_ref[:, cols]


def attention_kernel(
    first,
    parity_ref,
    query_ref,
    gradient_ref,
    key_own_ref,
    value_own_ref,
    key_one_ref,
    value_one_ref,
    key_even_ref,
    value_even_ref,
    key_odd_ref,
    value_odd_ref,
    query_up_ref,
    value_up_ref,
    query_low_ref,
    query_low_t_ref,
    cos_ref,
    sin_ref,
    value_low_ref,
    bias_ref,
    *rest,
):
    if first:
        out_ref, up_query_ref, up_value_ref, query_back_ref, value_back_ref, key_buf, value_buf = rest
    else:
        (_, query_back_in, value_back_in) = rest[:3]
        out_ref, up_query_ref, up_value_ref, query_back_ref, value_back_ref, key_buf, value_buf = rest[3:]
    tokens = query_ref.shape[0]

    @pl.when(pl.program_id(0) == 0)
    def _():
        key_buf[:, HEAD_SIZE:] = bias_ref[...]
        value_buf[:, HEAD_SIZE:] = value_low_ref[...]
        if first:
            query_back_ref[...] = jnp.zeros_like(query_back_ref)
            value_back_ref[...] = jnp.zeros_like(value_back_ref)
        else:
            query_back_ref[...] = query_back_in[...]
            value_back_ref[...] = value_back_in[...]

    odd = parity_ref[0] == 1
    key_buf[0:tokens, :HEAD_SIZE] = jnp.where(odd, key_odd_ref[...], key_even_ref[...])
    key_buf[tokens : 2 * tokens, :HEAD_SIZE] = key_one_ref[...]
    key_buf[2 * tokens :, :HEAD_SIZE] = key_own_ref[...]
    value_buf[0:tokens, :HEAD_SIZE] = jnp.where(odd, value_odd_ref[...], value_even_ref[...])
    value_buf[tokens : 2 * tokens, :HEAD_SIZE] = value_one_ref[...]
    value_buf[2 * tokens :, :HEAD_SIZE] = value_own_ref[...]

    query_up = query_up_ref[...]
    value_up = value_up_ref[...]
    value_up_pad = jnp.concatenate(
        [value_up, jnp.zeros((LANES - RANK, HEAD_SIZE), jnp.bfloat16)], axis=0
    )
    rows = GROUPS * SUB
    row = lax.broadcasted_iota(jnp.int32, (rows, LANES), 0)
    lane = lax.broadcasted_iota(jnp.int32, (rows, LANES), 1)
    second = (row % SUB) // BLOCK == 1
    lower = lane <= row % BLOCK
    extent = KEYS // BLOCK
    limits = {
        0: ~lower,
        1: ~lower | ~second,
        extent - 2: lower | second,
        extent - 1: lower,
    }

    up_query = jnp.zeros((RANK, GROUP_WIDTH), jnp.float32)
    up_value = jnp.zeros((HEAD_SIZE, HEAD_SIZE), jnp.float32)
    for step in range(tokens // SUB):
        own = pl.ds(step * SUB, SUB)
        window = pl.ds(step * SUB, KEYS)
        cosines = cos_ref[own, :]
        sines = sin_ref[own, :]
        adapted = query_ref[own, :].astype(jnp.float32) + mm(query_low_ref[own, :], query_up)
        turned = []
        for head in range(GROUPS):
            part = adapted[:, head * HEAD_SIZE : (head + 1) * HEAD_SIZE]
            turned.append(part * cosines + swap_halves(part) * sines)
        queries = (jnp.concatenate(turned, axis=0) * (SCORE_SCALE * LOG2_E)).astype(jnp.bfloat16)
        block_of = (row % SUB) // BLOCK + step * (SUB // BLOCK)
        chosen = (lane == block_of).astype(jnp.float32).astype(jnp.bfloat16)
        queries = jnp.concatenate([queries, chosen], axis=1)
        gradient = jnp.concatenate(
            [gradient_ref[own, head * HEAD_SIZE : (head + 1) * HEAD_SIZE] for head in range(GROUPS)],
            axis=0,
        )

        scores = mm(queries, key_buf[window, :], BOTH_MINOR)
        blocks = []
        for block in range(extent):
            part = scores[:, block * BLOCK : (block + 1) * BLOCK]
            if block in limits:
                part = jnp.where(limits[block], part, FORBIDDEN)
            blocks.append(part)
        highest = blocks[0]
        for part in blocks[1:]:
            highest = jnp.maximum(highest, part)
        highest = jnp.max(highest, axis=1, keepdims=True)
        weights = jnp.concatenate(
            [jnp.exp2(part - highest).astype(jnp.bfloat16) for part in blocks], axis=1
        )
        products = mm(weights, value_buf[window, :])
        total = products[:, HEAD_SIZE + RANK : HEAD_SIZE + RANK + 1]
        inverse = 1.0 / total
        low_part = (products[:, HEAD_SIZE:] * inverse).astype(jnp.bfloat16)
        outputs = (products[:, :HEAD_SIZE] * inverse + mm(low_part, value_up_pad)).astype(jnp.bfloat16)
        for head in range(GROUPS):
            out_ref[own, head * HEAD_SIZE : (head + 1) * HEAD_SIZE] = outputs[
                head * SUB : (head + 1) * SUB, :
            ]
        delta = jnp.sum(
            outputs.astype(jnp.float32) * gradient.astype(jnp.float32), axis=1, keepdims=True
        )
        up_value += mm(low_part, gradient, BOTH_MAJOR)

        gradient_low = mm(gradient, value_up_pad, BOTH_MINOR)
        grad_weights = mm(
            jnp.concatenate([gradient, gradient_low.astype(jnp.bfloat16)], axis=1),
            value_buf[window, :],
            BOTH_MINOR,
        )
        grad_scores = weights * (grad_weights - delta).astype(jnp.bfloat16)
        query_sums = mm(grad_scores, key_buf[window, :HEAD_SIZE]) * (inverse * SCORE_SCALE)
        turned = []
        for head in range(GROUPS):
            part = query_sums[head * SUB : (head + 1) * SUB, :]
            turned.append(part * cosines - swap_halves(part) * sines)
        query_grad = jnp.concatenate(turned, axis=1).astype(jnp.bfloat16)
        up_query += mm(query_low_t_ref[:, own], query_grad)
        query_back_ref[:, own] += mm(query_up, query_grad, BOTH_MINOR)
        spread = jnp.transpose(gradient_low * inverse)[:RANK, :].astype(jnp.bfloat16)
        value_back_ref[:, window] += mm(spread, weights)
    up_query_ref[...] = up_query
    up_value_ref[...] = up_value[:RANK, :]


def attention_chunk(first, last, parity, query_base, gradient, own, one, even, odd, shared, carried):
    count = last - first
    tokens = query_base.shape[0]
    keys = 3 * tokens
    wide = pl.BlockSpec((tokens, GROUP_WIDTH), lambda i, s: (0, first + i))
    near = pl.BlockSpec((tokens, HEAD_SIZE), lambda i, s: (0, i))
    far = pl.BlockSpec((tokens, HEAD_SIZE), lambda i, s: (0, count + i))

    def whole(rows, cols):
        return pl.BlockSpec((rows, cols), lambda i, s: (0, 0))

    query_up, value_up, query_low, query_low_t, cosines, sines, value_low, bias = shared
    in_specs = [
        wide,
        wide,
        *([near, far] * 4),
        pl.BlockSpec((RANK, GROUP_WIDTH), lambda i, s: (0, first + i)),
        pl.BlockSpec((RANK, HEAD_SIZE), lambda i, s: (0, first + i)),
        whole(tokens, RANK),
        whole(RANK, tokens),
        whole(tokens, HEAD_SIZE),
        whole(tokens, HEAD_SIZE),
        whole(keys, LANES),
        whole(keys, LANES),
    ]
    arguments = [
        query_base,
        gradient,
        own,
        own,
        one,
        one,
        even,
        even,
        odd,
        odd,
        query_up,
        value_up,
        query_low,
        query_low_t,
        cosines,
        sines,
        value_low,
        bias,
    ]
    aliases = {}
    if carried is not None:
        in_specs += [pl.BlockSpec(memory_space=pl.ANY), whole(RANK, tokens), whole(RANK, keys)]
        arguments += list(carried)
        aliases = {1 + len(arguments) - 3: 0}
    return pl.pallas_call(
        functools.partial(attention_kernel, carried is None),
        grid_spec=pltpu.PrefetchScalarGridSpec(
            num_scalar_prefetch=1,
            grid=(count,),
            in_specs=in_specs,
            out_specs=[
                wide,
                pl.BlockSpec((RANK, GROUP_WIDTH), lambda i, s: (0, i)),
                pl.BlockSpec((RANK, HEAD_SIZE), lambda i, s: (0, i)),
                whole(RANK, tokens),
                whole(RANK, keys),
            ],
            scratch_shapes=[
                pltpu.VMEM((keys, HEAD_SIZE + LANES), jnp.bfloat16),
                pltpu.VMEM((keys, HEAD_SIZE + LANES), jnp.bfloat16),
            ],
        ),
        out_shape=[
            jax.ShapeDtypeStruct(query_base.shape, jnp.bfloat16),
            jax.ShapeDtypeStruct((RANK, count * GROUP_WIDTH), jnp.float32),
            jax.ShapeDtypeStruct((RANK, count * HEAD_SIZE), jnp.float32),
            jax.ShapeDtypeStruct((RANK, tokens), jnp.float32),
            jax.ShapeDtypeStruct((RANK, keys), jnp.float32),
        ],
        input_output_aliases=aliases,
        compiler_params=pltpu.CompilerParams(vmem_limit_bytes=50 * 2**20),
    )(parity, *arguments)


def head_sum(x):
    if lax.axis_size("head") == 2:
        return x + lax.ppermute(x, "head", [(0, 1), (1, 0)])
    return lax.psum(x, "head")


def mask_bias(block_mask, device_index, mask_height):
    band = block_mask.shape[1]
    own_mask = lax.dynamic_slice_in_dim(block_mask, device_index * mask_height, mask_height, 0)
    reach = WINDOW // BLOCK
    key_blocks = jnp.arange(mask_height + reach, dtype=jnp.int32)
    offset = reach + jnp.arange(mask_height, dtype=jnp.int32)[None, :] - key_blocks[:, None]
    hit = jnp.any(
        (offset[:, :, None] == jnp.arange(band, dtype=jnp.int32)[None, None, :])
        & (own_mask[None, :, :] == 1),
        axis=-1,
    )
    real = device_index * mask_height - reach + key_blocks >= 0
    bias = jnp.where(hit & real[:, None], 0.0, FORBIDDEN).astype(jnp.bfloat16)
    bias = jnp.pad(bias, ((0, 0), (0, LANES - mask_height)))
    return jnp.repeat(bias, BLOCK, axis=0)


def per_device(
    hidden_states,
    query_base,
    key_base,
    frozen_value_rows,
    query_down,
    query_up,
    value_down,
    value_up_weight,
    positions,
    block_mask,
    output_gradient,
):
    tokens = hidden_states.shape[0]
    devices = lax.axis_size("ctx")
    device_index = lax.axis_index("ctx")
    kv_heads = key_base.shape[1] // HEAD_SIZE
    forward_one = [(i, i + 1) for i in range(devices - 1)]
    even_two = [(i, i + 2) for i in range(0, devices - 2, 2)]
    even_one = [(i, i + 1) for i in range(0, devices - 1, 2)]

    half = HEAD_SIZE // 2
    frequency = ROPE_BASE ** (-(2.0 * jnp.arange(half, dtype=jnp.float32)) / HEAD_SIZE)
    frequency = jnp.concatenate([frequency, frequency])[None, :]
    cosines, sines, *packed = pl.pallas_call(
        functools.partial(prologue_kernel, CHUNKS),
        out_shape=[
            jax.ShapeDtypeStruct((tokens, HEAD_SIZE), jnp.float32),
            jax.ShapeDtypeStruct((tokens, HEAD_SIZE), jnp.float32),
            *(
                jax.ShapeDtypeStruct((tokens, 2 * (last - first) * HEAD_SIZE), jnp.bfloat16)
                for first, last in CHUNKS
            ),
        ],
        compiler_params=pltpu.CompilerParams(vmem_limit_bytes=50 * 2**20),
    )(positions[:, None], frequency, key_base, frozen_value_rows)

    both_down = jnp.concatenate([query_down, value_down], axis=1)
    low = head_sum(mm(both_down, hidden_states, (((0,), (1,)), ((), ())))).astype(jnp.bfloat16)
    query_low_t = low[:RANK]
    value_low_t = low[RANK:]
    low_one = lax.ppermute(value_low_t, "ctx", forward_one)
    low_two = lax.ppermute(value_low_t, "ctx", [(i, i + 2) for i in range(devices - 2)])
    value_low = jnp.concatenate([low_two, low_one, value_low_t], axis=1)
    value_low = jnp.concatenate(
        [
            value_low,
            jnp.ones((1, 3 * tokens), jnp.bfloat16),
            jnp.zeros((LANES - RANK - 1, 3 * tokens), jnp.bfloat16),
        ],
        axis=0,
    ).T
    bias = mask_bias(block_mask, device_index, tokens // BLOCK)
    parity = (device_index % 2).astype(jnp.int32).reshape(1)

    ones, evens, odds = [], [], []
    for own in packed:
        ones.append(lax.ppermute(own, "ctx", forward_one))
        evens.append(lax.ppermute(own, "ctx", even_two))
    for one in ones:
        odds.append(lax.ppermute(one, "ctx", even_one))

    shared = (
        query_up,
        value_up_weight,
        query_low_t.T,
        query_low_t,
        cosines,
        sines,
        value_low,
        bias,
    )
    carried = None
    up_queries, up_values = [], []
    for chunk, (first, last) in enumerate(CHUNKS):
        attention_out, up_query, up_value, query_back, value_back = attention_chunk(
            first,
            last,
            parity,
            query_base,
            output_gradient,
            packed[chunk],
            ones[chunk],
            evens[chunk],
            odds[chunk],
            shared,
            carried,
        )
        carried = (attention_out, query_back, value_back)
        up_queries.append(up_query)
        up_values.append(up_value)

    back_one = lax.ppermute(
        value_back[:, tokens : 2 * tokens], "ctx", [(i + 1, i) for i in range(devices - 1)]
    )
    back_two = lax.ppermute(value_back[:, :tokens], "ctx", [(i + 2, i) for i in range(devices - 2)])
    value_back = value_back[:, 2 * tokens :] + back_one + back_two
    back = head_sum(jnp.concatenate([query_back, value_back], axis=0)).astype(jnp.bfloat16)
    down = mm(back, hidden_states)
    features = down.shape[1]
    partial = jnp.concatenate([down[:RANK], down[RANK:], *up_queries, *up_values], axis=1)
    columns = partial.shape[1]
    piece = -(-columns // (devices * LANES)) * LANES
    partial = jnp.pad(partial.astype(jnp.bfloat16), ((0, 0), (0, devices * piece - columns)))
    partial = partial.reshape(RANK, devices, piece).transpose(1, 0, 2)
    received = lax.all_to_all(partial, "ctx", 0, 0)
    mine = jnp.sum(received.astype(jnp.float32), axis=0) * ((devices * tokens) ** (-0.5))
    mine = jnp.broadcast_to(mine.astype(jnp.bfloat16)[None], (devices, RANK, piece))
    summed = lax.all_to_all(mine, "ctx", 0, 0)
    summed = summed.transpose(1, 0, 2).reshape(RANK, devices * piece).astype(jnp.float32)
    query_columns = kv_heads * GROUP_WIDTH
    up_first = 2 * features
    return (
        attention_out,
        summed[:, :features].T,
        summed[:, up_first : up_first + query_columns],
        summed[:, features:up_first].T,
        summed[:, up_first + query_columns : columns],
    )


def solution(mesh):
    placed = (
        P("ctx", "head"),
        P("ctx", "head"),
        P("ctx", "head"),
        P("ctx", "head"),
        P("head", None),
        P(None, "head"),
        P("head", None),
        P(None, "head"),
        P("ctx"),
        P(),
        P("ctx", "head"),
    )
    return jax.shard_map(
        per_device,
        mesh=mesh,
        in_specs=placed,
        out_specs=(
            P("ctx", "head"),
            P("head", None),
            P(None, "head"),
            P("head", None),
            P(None, "head"),
        ),
        check_vma=False,
    )
```

time: 595 us -> 190 us (0.32); the launches traced: 587 us -> 189 us
  matrix products: 180 us -> 3.04 us
  waiting for transfers between devices: 144 us -> 10 us
  other arithmetic: 117 us -> 6.87 us
  local copies, waits for them, and re-layouts: 94.5 us -> 18.8 us
  Pallas kernels: 0 us -> 67 us
  starting transfers between devices: 17.6 us -> 52 us
  between operations: 14.6 us -> 0.89 us
  blocking collectives: 17.8 us -> 30.5 us
    dot_general x50 -> x2, matrix products: 180 us -> 3.04 us  [mm(): lax.dot_general(left, right, dims, preferred_element_type=jnp.float32)]
    psum x1 -> x0, waiting for transfers between devices: 87.2 us -> none  [per_device(): summed = lax.psum((down_query, up_query, down_value, up_value), 'ctx')]
    pallas_call x0 -> x4, Pallas kernels: none -> 67 us  [the longest x3 63.1 us: attention_chunk(): pl.pallas_call(functools.partial(attention_kernel, carried is None), grid...]
    ppermute x6 -> x15, waiting for transfers between devices: 57.3 us -> 10 us  [the longest x1 4.2 us: per_device(): lax.ppermute(value_back[:, :tokens], 'ctx', [(i + 2, i) for i in range(de...]
    and x16 -> x0, other arithmetic: 38.9 us -> none  [allowed_pairs(): return token_ok & spread_out]
    ppermute x6 -> x15, starting transfers between devices: 17.6 us -> 52 us  [the longest x3 14.6 us: per_device(): evens.append(lax.ppermute(own, 'ctx', even_two))]
    all_to_all x0 -> x2, blocking collectives: none -> 30.5 us  [the longest x1 16.4 us: per_device(): received = lax.all_to_all(partial, 'ctx', 0, 0)]
    reduce_sum x16 -> x1, other arithmetic: 24.5 us -> 0.05 us  [per_device(): jnp.sum(received.astype(jnp.float32), axis=0) * (devices * tokens) ** (-0.5)]
  transfers between devices with their start and end apart: 7 -> 15, of which waited for: 3 -> 5; matrix products, arithmetic and copies ran while one was open for 11% -> 9% of each run, Pallas kernels for 0% -> 25%
where the time goes in v1:
time: 190 us; the launch traced here: 189 us
  Pallas kernels  67 us (35%)
  starting transfers between devices  52 us (27%)
  blocking collectives  30.5 us (16%)
  local copies, waits for them, and re-layouts  18.8 us (10%)
  waiting for transfers between devices  10 us (5%)
  other arithmetic  6.87 us (4%)
  matrix products  3.04 us (2%)
    pallas_call x3, Pallas kernels, attention_chunk(): pl.pallas_call(functools.partial(attention_kernel, carried is None), grid...  63.1 us
    all_to_all x1, blocking collectives, per_device(): received = lax.all_to_all(partial, 'ctx', 0, 0)  16.4 us
    ppermute x3, starting transfers between devices, per_device(): evens.append(lax.ppermute(own, 'ctx', even_two))  14.6 us
    all_to_all x1, blocking collectives, per_device(): summed = lax.all_to_all(mine, 'ctx', 0, 0)  14.1 us
    ppermute x1, starting transfers between devices, per_device(): low_one = lax.ppermute(value_low_t, 'ctx', forward_one)  13.5 us
    ppermute x3, starting transfers between devices, per_device(): ones.append(lax.ppermute(own, 'ctx', forward_one))  8.66 us
    unnamed x33, local copies, waits for them, and re-layouts  8 us
    ppermute x3, starting transfers between devices, per_device(): odds.append(lax.ppermute(one, 'ctx', even_one))  6.47 us
  transfers between devices with their start and end apart: 15, of which 5 were waited for; matrix products, arithmetic and copies ran while one was open for 9% of the time, Pallas kernels for 25%

profile of v1, /device:TPU:0, one launch (start us, length us, event | category | flops | bytes accessed | tf_op | source)
XLA Modules:
  0.0 189.2 jit_solution(3461928722298097712)
XLA Ops:
  0.7 1.7 copy.46.positions_ref
  4.6 3.9 %shard_map.146 = (f32[512,128]{1,0:T(8,128)S(1)}, f32[512,128]{1,0:T(8,128)S(1)}, bf16[512,768]{1,0:T(8,128)(2,1)}, bf16[512,768]{1,0:T(8,128)(2,1)S(1)}, bf16[512,512]{1,0:T(8,128)(2,1)}) custom-call(s32[512,1]{1,0:T(8,128)S(1)} %copy-done.8, f32[1,128]{1,0:T(1,128)S(1)} %maximum_bitcast_fusion.1.frequency_ref, bf16[512,1024]{1,0:T(8,128)(2,1)S(1)} %copy-done.7, ...), custom_call_target="tpu_custom_call" | custom-call | tf_op jit(solution)/shard_map/pallas_call | solution.py:325
  8.5 3.3 %collective-permute-start.9 = (bf16[512,768]{1,0:T(8,128)(2,1)}, bf16[512,768]{1,0:T(8,128)(2,1)}, u32[]{:S(2)}, u32[]{:S(2)}) collective-permute-start(bf16[512,768]{1,0:T(8,128)(2,1)} %get-tuple-element.29.key_own_ref.value_own_ref), channel_id=1, source_target_pairs={{0,2},{2,4},{4,6},{6,8},{8,10},{10,12},{12,14},{14,16},{16,18},{18... | collective-permute-start | bytes 2359304 | tf_op jit(solution)/shard_map/ppermute | solution.py:358
  11.8 4.4 %collective-permute-start.10 = (bf16[512,768]{1,0:T(8,128)(2,1)}, bf16[512,768]{1,0:T(8,128)(2,1)}, u32[]{:S(2)}, u32[]{:S(2)}) collective-permute-start(bf16[512,768]{1,0:T(8,128)(2,1)} %get-tuple-element.29.key_own_ref.value_own_ref), channel_id=1, source_target_pairs={{0,4},{4,8},{8,12},{12,16},{16,20},{20,24},{24,28},{1,5},{5,9},{9,... | collective-permute-start | bytes 2359304 | tf_op jit(solution)/shard_map/ppermute | solution.py:359
  16.2 2.5 %fusion = f32[32,512]{1,0:T(8,128)} fusion(bf16[512,2688]{1,0:T(8,128)(2,1)S(1)} %copy-done, bf16[2688,16]{0,1:T(8,128)(2,1)} %param.17, bf16[2688,16]{0,1:T(8,128)(2,1)} %param.15), kind=kOutput, calls=%fused_computation.7 | convolution fusion | flops 88424448 | bytes 2990080 | tf_op jit(solution)/shard_map/dot_general | solution.py:36
  18.7 1.5 collective-permute-start.3
  20.1 2.2 %collective-permute-start.6 = (bf16[512,768]{1,0:T(8,128)(2,1)S(1)}, bf16[512,768]{1,0:T(8,128)(2,1)}, u32[]{:S(2)}, u32[]{:S(2)}) collective-permute-start(bf16[512,768]{1,0:T(8,128)(2,1)S(1)} %get-tuple-element.28.key_own_ref.value_own_ref), channel_id=1, source_target_pairs={{0,2},{2,4},{4,6},{6,8},{8,10},{10,12},{12,14},{14,16},{16,18},{18... | collective-permute-start | bytes 2359304 | tf_op jit(solution)/shard_map/ppermute | solution.py:358
  22.4 3.2 %collective-permute-start = (bf16[512,512]{1,0:T(8,128)(2,1)}, bf16[512,512]{1,0:T(8,128)(2,1)}, u32[]{:S(2)}, u32[]{:S(2)}) collective-permute-start(bf16[512,512]{1,0:T(8,128)(2,1)} %get-tuple-element.25.key_own_ref.value_own_ref), channel_id=1, source_target_pairs={{0,2},{2,4},{4,6},{6,8},{8,10},{10,12},{12,14},{14,16},{16,18},{18... | collective-permute-start | bytes 1572872 | tf_op jit(solution)/shard_map/ppermute | solution.py:358
  27.8 3.2 %collective-permute-start.4 = (bf16[16,512]{1,0:T(8,128)(2,1)}, bf16[16,512]{1,0:T(8,128)(2,1)}, u32[]{:S(2)}, u32[]{:S(2)}) collective-permute-start(bf16[16,512]{1,0:T(8,128)(2,1)} %get-tuple-element.49), channel_id=1, source_target_pairs={{0,4},{2,6},{4,8},{6,10},{8,12},{10,14},{12,16},{14,18},{16,20},{1... | collective-permute-start | bytes 49160 | tf_op jit(solution)/shard_map/ppermute | solution.py:343
  31.0 1.3 fusion.5
  32.3 1.5 collective-permute-done.4
  33.8 13.5 %collective-permute-start.5 = (bf16[16,512]{1,0:T(8,128)(2,1)}, bf16[16,512]{1,0:T(8,128)(2,1)S(1)}, u32[]{:S(2)}, u32[]{:S(2)}) collective-permute-start(bf16[16,512]{1,0:T(8,128)(2,1)} %get-tuple-element.49), channel_id=1, source_target_pairs={{0,2},{2,4},{4,6},{6,8},{8,10},{10,12},{12,14},{14,16},{16,18},{18... | collective-permute-start | bytes 49160 | tf_op jit(solution)/shard_map/ppermute | solution.py:342
  48.4 5.2 %collective-permute-start.7 = (bf16[512,768]{1,0:T(8,128)(2,1)S(1)}, bf16[512,768]{1,0:T(8,128)(2,1)}, u32[]{:S(2)}, u32[]{:S(2)}) collective-permute-start(bf16[512,768]{1,0:T(8,128)(2,1)S(1)} %get-tuple-element.28.key_own_ref.value_own_ref), channel_id=1, source_target_pairs={{0,4},{4,8},{8,12},{12,16},{16,20},{20,24},{24,28},{1,5},{5,9},{9,... | collective-permute-start | bytes 2359304 | tf_op jit(solution)/shard_map/ppermute | solution.py:359
  53.6 2.2 %collective-permute-start.11 = (bf16[512,768]{1,0:T(8,128)(2,1)}, bf16[512,768]{1,0:T(8,128)(2,1)}, u32[]{:S(2)}, u32[]{:S(2)}) collective-permute-start(bf16[512,768]{1,0:T(8,128)(2,1)} %collective-permute-done.9.key_one_ref.value_one_ref), channel_id=1, source_target_pairs={{0,2},{4,6},{8,10},{12,14},{16,18},{20,22},{24,26},{28,30},{1,3},{... | collective-permute-start | bytes 2359304 | tf_op jit(solution)/shard_map/ppermute | solution.py:361
  55.8 2.2 %collective-permute-start.8 = (bf16[512,768]{1,0:T(8,128)(2,1)}, bf16[512,768]{1,0:T(8,128)(2,1)}, u32[]{:S(2)}, u32[]{:S(2)}) collective-permute-start(bf16[512,768]{1,0:T(8,128)(2,1)} %collective-permute-done.6.key_one_ref.value_one_ref), channel_id=1, source_target_pairs={{0,2},{4,6},{8,10},{12,14},{16,18},{20,22},{24,26},{28,30},{1,3},{... | collective-permute-start | bytes 2359304 | tf_op jit(solution)/shard_map/ppermute | solution.py:361
  59.2 1.4 copy.54
  60.5 1.3 pad.8.clone
  63.0 1.5 copy.51.query_low_ref
  64.5 5.0 %collective-permute-start.1 = (bf16[512,512]{1,0:T(8,128)(2,1)}, bf16[512,512]{1,0:T(8,128)(2,1)}, u32[]{:S(2)}, u32[]{:S(2)}) collective-permute-start(bf16[512,512]{1,0:T(8,128)(2,1)} %get-tuple-element.25.key_own_ref.value_own_ref), channel_id=1, source_target_pairs={{0,4},{4,8},{8,12},{12,16},{16,20},{20,24},{24,28},{1,5},{5,9},{9,... | collective-permute-start | bytes 1572872 | tf_op jit(solution)/shard_map/ppermute | solution.py:359
  69.4 2.1 %collective-permute-start.2 = (bf16[512,512]{1,0:T(8,128)(2,1)}, bf16[512,512]{1,0:T(8,128)(2,1)}, u32[]{:S(2)}, u32[]{:S(2)}) collective-permute-start(bf16[512,512]{1,0:T(8,128)(2,1)} %collective-permute-done.key_one_ref.value_one_ref), channel_id=1, source_target_pairs={{0,2},{4,6},{8,10},{12,14},{16,18},{20,22},{24,26},{28,30},{1,3},{... | collective-permute-start | bytes 1572872 | tf_op jit(solution)/shard_map/ppermute | solution.py:361
  71.5 1.4 pad_maximum_fusion.1
  72.9 1.7 copy.47
  80.9 23.5 %shard_map.147 = (bf16[512,2048]{1,0:T(8,128)(2,1)}, f32[16,768]{1,0:T(8,128)S(1)}, f32[16,384]{1,0:T(8,128)S(1)}, f32[16,512]{1,0:T(8,128)S(1)}, f32[16,1536]{1,0:T(8,128)S(1)}) custom-call(s32[1]{0:T(128)} %bitcast.parity_ref, bf16[512,2048]{1,0:T(8,128)(2,1)} %query_ref.5, bf16[512,2048]{1,0:T(8,128)(2,1)} %gradient_ref.5, ...), custom_call_target="tpu_custom_call" | custom-call | tf_op jit(solution)/shard_map/pallas_call | solution.py:248
  104.4 23.3 %shard_map.148 = (bf16[512,2048]{1,0:T(8,128)(2,1)}, f32[16,768]{1,0:T(8,128)S(1)}, f32[16,384]{1,0:T(8,128)S(1)}, f32[16,512]{1,0:T(8,128)S(1)}, f32[16,1536]{1,0:T(8,128)S(1)}) custom-call(s32[1]{0:T(128)} %bitcast.parity_ref, bf16[512,2048]{1,0:T(8,128)(2,1)} %query_ref.5, bf16[512,2048]{1,0:T(8,128)(2,1)} %gradient_ref.5, ...), custom_call_target="tpu_custom_call", output_to_operand_aliasing={{0}: (19, {})} | custom-call | tf_op jit(solution)/shard_map/pallas_call | solution.py:248
  127.7 16.3 %shard_map.149 = (bf16[512,2048]{1,0:T(8,128)(2,1)}, f32[16,512]{1,0:T(8,128)S(1)}, f32[16,256]{1,0:T(8,128)S(1)}, f32[16,512]{1,0:T(8,128)S(1)}, f32[16,1536]{1,0:T(8,128)S(1)}) custom-call(s32[1]{0:T(128)} %bitcast.parity_ref, bf16[512,2048]{1,0:T(8,128)(2,1)} %query_ref.5, bf16[512,2048]{1,0:T(8,128)(2,1)} %gradient_ref.5, ...), custom_call_target="tpu_custom_call", output_to_operand_aliasing={{0}: (19, {})} | custom-call | tf_op jit(solution)/shard_map/pallas_call | solution.py:248
  144.0 1.3 collective-permute-start.12
  145.3 1.3 collective-permute-start.13
  147.1 4.2 %collective-permute-done.13 = f32[16,512]{1,0:T(8,128)S(1)} collective-permute-done((f32[16,512]{1,0:T(8,128)S(1)}, f32[16,512]{1,0:T(8,128)S(1)}, u32[]{:S(2)}, u32[]{:S(2)}) %collective-permute-start.13) | collective-permute-done | bytes 32800 | tf_op jit(solution)/shard_map/ppermute | solution.py:396
  151.3 1.6 collective-permute-start.14
  152.9 2.8 %collective-permute-done.14 = f32[32,512]{1,0:T(8,128)S(1)} collective-permute-done((f32[32,512]{1,0:T(8,128)S(1)}, f32[32,512]{1,0:T(8,128)S(1)}, u32[]{:S(2)}, u32[]{:S(2)}) %collective-permute-start.14) | collective-permute-done | bytes 65568 | tf_op jit(solution)/shard_map/ppermute | solution.py:280
  156.4 16.4 %all_to_all.10 = bf16[16,16,640]{2,1,0:T(8,128)(2,1)S(1)} all-to-all(bf16[16,16,640]{2,1,0:T(8,128)(2,1)S(1)} %bitcast.34), channel_id=1, replica_groups=mesh['ctx'=16,'head'=2] {'ctx'}, dimensions={0} | all-to-all | bytes 655360 | tf_op jit(solution)/shard_map/all_to_all | solution.py:406
  172.9 14.1 %all_to_all.11 = bf16[16,16,640]{2,1,0:T(8,128)(2,1)S(1)} all-to-all(bf16[16,16,640]{2,1,0:T(8,128)(2,1)S(1)} %broadcast_in_dim.42), channel_id=1, replica_groups=mesh['ctx'=16,'head'=2] {'ctx'}, dimensions={0} | all-to-all | bytes 655360 | tf_op jit(solution)/shard_map/all_to_all | solution.py:409
  (78 shorter events, 17.6 us)
Async XLA Ops:
  0.6 15.5 %copy-start = (bf16[512,2688]{1,0:T(8,128)(2,1)S(1)}, bf16[512,2688]{1,0:T(8,128)(2,1)}, u32[]{:S(2)}) copy-start(bf16[512,2688]{1,0:T(8,128)(2,1)} %param.11) | copy-start | bytes 8257540
  2.4 1.2 copy-start.7
  3.6 0.9 copy-start.8
  4.6 21.6 %copy-start.14 = (s32[64,9]{0,1:T(8,128)S(1)}, s32[64,9]{0,1:T(8,128)}, u32[]{:S(2)}) copy-start(s32[64,9]{0,1:T(8,128)} %param.20) | copy-start | bytes 6916
  8.5 11.6 %copy-start.1 = (f32[512,128]{1,0:T(8,128)}, f32[512,128]{1,0:T(8,128)S(1)}, u32[]{:S(2)}) copy-start(f32[512,128]{1,0:T(8,128)S(1)} %get-tuple-element.26.cos_ref) | copy-start | bytes 786436
  8.5 11.6 %copy-start.3 = (f32[512,128]{1,0:T(8,128)}, f32[512,128]{1,0:T(8,128)S(1)}, u32[]{:S(2)}) copy-start(f32[512,128]{1,0:T(8,128)S(1)} %get-tuple-element.27.sin_ref) | copy-start | bytes 786436
  8.5 45.1 %collective-permute-start.9 = (bf16[512,768]{1,0:T(8,128)(2,1)}, bf16[512,768]{1,0:T(8,128)(2,1)}, u32[]{:S(2)}, u32[]{:S(2)}) collective-permute-start(bf16[512,768]{1,0:T(8,128)(2,1)} %get-tuple-element.29.key_own_ref.value_own_ref), channel_id=1, source_target_pairs={{0,2},{2,4},{4,6},{6,8},{8,10},{10,12},{12,14},{14,16},{16,18},{18... | collective-permute-start | bytes 2359304 | tf_op jit(solution)/shard_map/ppermute | solution.py:358
  11.8 57.6 %collective-permute-start.10 = (bf16[512,768]{1,0:T(8,128)(2,1)}, bf16[512,768]{1,0:T(8,128)(2,1)}, u32[]{:S(2)}, u32[]{:S(2)}) collective-permute-start(bf16[512,768]{1,0:T(8,128)(2,1)} %get-tuple-element.29.key_own_ref.value_own_ref), channel_id=1, source_target_pairs={{0,4},{4,8},{8,12},{12,16},{16,20},{20,24},{24,28},{1,5},{5,9},{9,... | collective-permute-start | bytes 2359304 | tf_op jit(solution)/shard_map/ppermute | solution.py:359
  18.7 7.6 %collective-permute-start.3 = (f32[32,512]{1,0:T(8,128)}, f32[32,512]{1,0:T(8,128)}, u32[]{:S(2)}, u32[]{:S(2)}) collective-permute-start(f32[32,512]{1,0:T(8,128)} %fusion), channel_id=1, source_target_pairs={{0,1},{1,0},{2,3},{3,2},{4,5},{5,4},{6,7},{7,6},{8,9},{9,8},{10,11... | collective-permute-start | bytes 196616 | tf_op jit(solution)/shard_map/ppermute | solution.py:280
  20.1 35.6 %collective-permute-start.6 = (bf16[512,768]{1,0:T(8,128)(2,1)S(1)}, bf16[512,768]{1,0:T(8,128)(2,1)}, u32[]{:S(2)}, u32[]{:S(2)}) collective-permute-start(bf16[512,768]{1,0:T(8,128)(2,1)S(1)} %get-tuple-element.28.key_own_ref.value_own_ref), channel_id=1, source_target_pairs={{0,2},{2,4},{4,6},{6,8},{8,10},{10,12},{12,14},{14,16},{16,18},{18... | collective-permute-start | bytes 2359304 | tf_op jit(solution)/shard_map/ppermute | solution.py:358
  22.4 42.1 %collective-permute-start = (bf16[512,512]{1,0:T(8,128)(2,1)}, bf16[512,512]{1,0:T(8,128)(2,1)}, u32[]{:S(2)}, u32[]{:S(2)}) collective-permute-start(bf16[512,512]{1,0:T(8,128)(2,1)} %get-tuple-element.25.key_own_ref.value_own_ref), channel_id=1, source_target_pairs={{0,2},{2,4},{4,6},{6,8},{8,10},{10,12},{12,14},{14,16},{16,18},{18... | collective-permute-start | bytes 1572872 | tf_op jit(solution)/shard_map/ppermute | solution.py:358
  27.8 6.1 %collective-permute-start.4 = (bf16[16,512]{1,0:T(8,128)(2,1)}, bf16[16,512]{1,0:T(8,128)(2,1)}, u32[]{:S(2)}, u32[]{:S(2)}) collective-permute-start(bf16[16,512]{1,0:T(8,128)(2,1)} %get-tuple-element.49), channel_id=1, source_target_pairs={{0,4},{2,6},{4,8},{6,10},{8,12},{10,14},{12,16},{14,18},{16,20},{1... | collective-permute-start | bytes 49160 | tf_op jit(solution)/shard_map/ppermute | solution.py:343
  33.8 14.5 %collective-permute-start.5 = (bf16[16,512]{1,0:T(8,128)(2,1)}, bf16[16,512]{1,0:T(8,128)(2,1)S(1)}, u32[]{:S(2)}, u32[]{:S(2)}) collective-permute-start(bf16[16,512]{1,0:T(8,128)(2,1)} %get-tuple-element.49), channel_id=1, source_target_pairs={{0,2},{2,4},{4,6},{6,8},{8,10},{10,12},{12,14},{14,16},{16,18},{18... | collective-permute-start | bytes 49160 | tf_op jit(solution)/shard_map/ppermute | solution.py:342
  48.4 7.4 %copy-start.13 = (bf16[16,512]{1,0:T(8,128)(2,1)}, bf16[16,512]{1,0:T(8,128)(2,1)S(1)}, u32[]{:S(2)}) copy-start(bf16[16,512]{1,0:T(8,128)(2,1)S(1)} %collective-permute-done.5) | copy-start | bytes 49156
  48.4 56.0 %collective-permute-start.7 = (bf16[512,768]{1,0:T(8,128)(2,1)S(1)}, bf16[512,768]{1,0:T(8,128)(2,1)}, u32[]{:S(2)}, u32[]{:S(2)}) collective-permute-start(bf16[512,768]{1,0:T(8,128)(2,1)S(1)} %get-tuple-element.28.key_own_ref.value_own_ref), channel_id=1, source_target_pairs={{0,4},{4,8},{8,12},{12,16},{16,20},{20,24},{24,28},{1,5},{5,9},{9,... | collective-permute-start | bytes 2359304 | tf_op jit(solution)/shard_map/ppermute | solution.py:359
  53.6 22.1 %collective-permute-start.11 = (bf16[512,768]{1,0:T(8,128)(2,1)}, bf16[512,768]{1,0:T(8,128)(2,1)}, u32[]{:S(2)}, u32[]{:S(2)}) collective-permute-start(bf16[512,768]{1,0:T(8,128)(2,1)} %collective-permute-done.9.key_one_ref.value_one_ref), channel_id=1, source_target_pairs={{0,2},{4,6},{8,10},{12,14},{16,18},{20,22},{24,26},{28,30},{1,3},{... | collective-permute-start | bytes 2359304 | tf_op jit(solution)/shard_map/ppermute | solution.py:361
  55.8 48.6 %collective-permute-start.8 = (bf16[512,768]{1,0:T(8,128)(2,1)}, bf16[512,768]{1,0:T(8,128)(2,1)}, u32[]{:S(2)}, u32[]{:S(2)}) collective-permute-start(bf16[512,768]{1,0:T(8,128)(2,1)} %collective-permute-done.6.key_one_ref.value_one_ref), channel_id=1, source_target_pairs={{0,2},{4,6},{8,10},{12,14},{16,18},{20,22},{24,26},{28,30},{1,3},{... | collective-permute-start | bytes 2359304 | tf_op jit(solution)/shard_map/ppermute | solution.py:361
  64.5 63.3 %collective-permute-start.1 = (bf16[512,512]{1,0:T(8,128)(2,1)}, bf16[512,512]{1,0:T(8,128)(2,1)}, u32[]{:S(2)}, u32[]{:S(2)}) collective-permute-start(bf16[512,512]{1,0:T(8,128)(2,1)} %get-tuple-element.25.key_own_ref.value_own_ref), channel_id=1, source_target_pairs={{0,4},{4,8},{8,12},{12,16},{16,20},{20,24},{24,28},{1,5},{5,9},{9,... | collective-permute-start | bytes 1572872 | tf_op jit(solution)/shard_map/ppermute | solution.py:359
  69.4 58.3 %collective-permute-start.2 = (bf16[512,512]{1,0:T(8,128)(2,1)}, bf16[512,512]{1,0:T(8,128)(2,1)}, u32[]{:S(2)}, u32[]{:S(2)}) collective-permute-start(bf16[512,512]{1,0:T(8,128)(2,1)} %collective-permute-done.key_one_ref.value_one_ref), channel_id=1, source_target_pairs={{0,2},{4,6},{8,10},{12,14},{16,18},{20,22},{24,26},{28,30},{1,3},{... | collective-permute-start | bytes 1572872 | tf_op jit(solution)/shard_map/ppermute | solution.py:361
  76.5 1.0 copy-start.2
  77.4 0.9 copy-start.4
  78.4 0.9 copy-start.5
  79.3 0.8 copy-start.9
  80.1 0.8 copy-start.11
  80.9 23.5 %copy-start.6 = (bf16[512,16]{1,0:T(8,128)(2,1)S(1)}, bf16[512,16]{1,0:T(8,128)(2,1)}, u32[]{:S(2)}) copy-start(bf16[512,16]{1,0:T(8,128)(2,1)} %copy.51.query_low_ref) | copy-start | bytes 49156
  80.9 23.5 %copy-start.10 = (bf16[16,2048]{1,0:T(8,128)(2,1)S(1)}, bf16[16,2048]{1,0:T(8,128)(2,1)}, u32[]{:S(2)}) copy-start(bf16[16,2048]{1,0:T(8,128)(2,1)} %query_up_ref.5) | copy-start | bytes 196612
  80.9 23.6 %copy-start.12 = (bf16[16,1024]{1,0:T(8,128)(2,1)S(1)}, bf16[16,1024]{1,0:T(8,128)(2,1)}, u32[]{:S(2)}) copy-start(bf16[16,1024]{1,0:T(8,128)(2,1)} %value_up_ref.5) | copy-start | bytes 98308
  144.0 3.1 %collective-permute-start.12 = (f32[16,512]{1,0:T(8,128)S(1)}, f32[16,512]{1,0:T(8,128)S(1)}, u32[]{:S(2)}, u32[]{:S(2)}) collective-permute-start(f32[16,512]{1,0:T(8,128)S(1)} %get-tuple-element.47), channel_id=1, source_target_pairs={{2,0},{4,2},{6,4},{8,6},{10,8},{12,10},{14,12},{16,14},{18,16},{20... | collective-permute-start | bytes 98312 | tf_op jit(solution)/shard_map/ppermute | solution.py:393
  145.3 6.0 %collective-permute-start.13 = (f32[16,512]{1,0:T(8,128)S(1)}, f32[16,512]{1,0:T(8,128)S(1)}, u32[]{:S(2)}, u32[]{:S(2)}) collective-permute-start(f32[16,512]{1,0:T(8,128)S(1)} %get-tuple-element.48), channel_id=1, source_target_pairs={{4,0},{6,2},{8,4},{10,6},{12,8},{14,10},{16,12},{18,14},{20,16},{2... | collective-permute-start | bytes 98312 | tf_op jit(solution)/shard_map/ppermute | solution.py:396
  151.3 4.3 %collective-permute-start.14 = (f32[32,512]{1,0:T(8,128)S(1)}, f32[32,512]{1,0:T(8,128)S(1)}, u32[]{:S(2)}, u32[]{:S(2)}) collective-permute-start(f32[32,512]{1,0:T(8,128)S(1)} %pad_maximum_fusion), channel_id=1, source_target_pairs={{0,1},{1,0},{2,3},{3,2},{4,5},{5,4},{6,7},{7,6},{8,9},{9,8},{10,11... | collective-permute-start | bytes 196616 | tf_op jit(solution)/shard_map/ppermute | solution.py:280

commit v2 on v1

v2 whole, which is shorter than its diff:
```python
import functools

import jax
import jax.numpy as jnp
import numpy as np
from jax import lax
from jax.experimental import pallas as pl
from jax.experimental.pallas import tpu as pltpu
from jax.sharding import PartitionSpec as P

D = 5376
QUERY_HEADS = 32
KEY_VALUE_HEADS = 16
HEAD_SIZE = 128
WINDOW = 1024
BLOCK = 128
GROUPS = QUERY_HEADS // KEY_VALUE_HEADS
GROUP_WIDTH = GROUPS * HEAD_SIZE
SCORE_SCALE = (D // QUERY_HEADS) ** (-0.5)
LOG2_E = 1.4426950408889634
ROPE_BASE = 10000.0
FORBIDDEN = -1e30
RANK = 16

SUB = 256
KEYS = SUB + WINDOW
LANES = 128
OFFSET_LANE = 64
ONES_LANE = RANK

CHUNKS = ((0, 2), (2, 4), (4, 6), (6, 8))

ROWS_BY_COLS = (((1,), (0,)), ((), ()))
BOTH_MINOR = (((1,), (1,)), ((), ()))
BOTH_MAJOR = (((0,), (0,)), ((), ()))


def mm(left, right, dims=ROWS_BY_COLS):
    return lax.dot_general(left, right, dims, preferred_element_type=jnp.float32)


def swap_halves(x):
    return pltpu.roll(x, HEAD_SIZE // 2, 1)


def prologue_kernel(chunks, positions_ref, frequency_ref, key_ref, value_ref, cos_ref, sin_ref, *outs):
    tokens = key_ref.shape[0]
    half = HEAD_SIZE // 2
    angles = frequency_ref[...] * positions_ref[...].astype(jnp.float32)
    both = jnp.transpose(jnp.concatenate([jnp.cos(angles), jnp.sin(angles)], axis=0))
    turned = swap_halves(both)
    low_half = lax.broadcasted_iota(jnp.int32, both.shape, 1) < half
    cosines = jnp.where(low_half, both, turned)
    sines = jnp.where(low_half, -turned, both)
    cos_ref[...] = cosines
    sin_ref[...] = sines
    own = pl.ds(0, tokens)
    for (first, last), out_ref in zip(chunks, outs):
        count = last - first
        for head in range(first, last):
            cols = pl.ds(head * HEAD_SIZE, HEAD_SIZE)
            key = key_ref[:, cols].astype(jnp.float32)
            rotated = key * cosines + swap_halves(key) * sines
            out_ref[own, pl.ds((head - first) * HEAD_SIZE, HEAD_SIZE)] = rotated.astype(jnp.bfloat16)
            out_ref[own, pl.ds((count + head - first) * HEAD_SIZE, HEAD_SIZE)] = value_ref[:, cols]


def attention_kernel(
    first,
    place_ref,
    mask_ref,
    query_ref,
    gradient_ref,
    key_own_ref,
    value_own_ref,
    key_one_ref,
    value_one_ref,
    key_even_ref,
    value_even_ref,
    key_odd_ref,
    value_odd_ref,
    query_up_ref,
    value_up_ref,
    query_low_ref,
    query_low_t_ref,
    cos_ref,
    sin_ref,
    low_own_ref,
    low_one_ref,
    low_even_ref,
    low_odd_ref,
    *rest,
):
    if not first:
        (_, query_back_in, value_back_in) = rest[:3]
        rest = rest[3:]
    out_ref, up_query_ref, up_value_ref, query_back_ref, value_back_ref = rest[:5]
    key_buf, value_buf, query_buf, gradient_buf, weight_buf, score_buf, product_buf = rest[5:]
    tokens = query_ref.shape[0]
    keys = key_buf.shape[0]
    steps = tokens // SUB
    tiles = keys // SUB
    step_tiles = KEYS // SUB
    rows = GROUPS * SUB
    odd = place_ref[1] == 1

    @pl.when(pl.program_id(0) == 0)
    def _():
        first_block = place_ref[0] * (tokens // BLOCK)
        reach = WINDOW // BLOCK
        lane = lax.broadcasted_iota(jnp.int32, (BLOCK, LANES), 1)
        for key_block in range(keys // BLOCK):
            extra = jnp.where(lane == OFFSET_LANE, 1.0, 0.0)
            exists = first_block + (key_block - reach) >= 0
            for block in range(tokens // BLOCK):
                offset = reach + block - key_block
                if 0 <= offset <= reach:
                    hit = (mask_ref[offset, first_block + block] == 1) & exists
                    term = jnp.where(hit, 0.0, FORBIDDEN)
                else:
                    term = FORBIDDEN
                extra = jnp.where(lane == block, term, extra)
            key_buf[key_block * BLOCK : (key_block + 1) * BLOCK, HEAD_SIZE:] = extra.astype(jnp.bfloat16)
        low_far = jnp.where(odd, low_odd_ref[...], low_even_ref[...])
        low = jnp.concatenate([low_far, low_one_ref[...], low_own_ref[...]], axis=1)
        low = jnp.concatenate(
            [
                low.astype(jnp.float32),
                jnp.ones((2, keys), jnp.float32),
                jnp.zeros((LANES - RANK - 2, keys), jnp.float32),
            ],
            axis=0,
        )
        value_buf[:, HEAD_SIZE:] = jnp.transpose(low).astype(jnp.bfloat16)
        if first:
            query_back_ref[...] = jnp.zeros_like(query_back_ref)
            value_back_ref[...] = jnp.zeros_like(value_back_ref)
        else:
            query_back_ref[...] = query_back_in[...]
            value_back_ref[...] = value_back_in[...]

    key_buf[0:tokens, :HEAD_SIZE] = jnp.where(odd, key_odd_ref[...], key_even_ref[...])
    key_buf[tokens : 2 * tokens, :HEAD_SIZE] = key_one_ref[...]
    key_buf[2 * tokens :, :HEAD_SIZE] = key_own_ref[...]
    value_buf[0:tokens, :HEAD_SIZE] = jnp.where(odd, value_odd_ref[...], value_even_ref[...])
    value_buf[tokens : 2 * tokens, :HEAD_SIZE] = value_one_ref[...]
    value_buf[2 * tokens :, :HEAD_SIZE] = value_own_ref[...]

    query_up = query_up_ref[...]
    value_up = jnp.concatenate(
        [value_up_ref[...], jnp.zeros((LANES - RANK, HEAD_SIZE), jnp.bfloat16)], axis=0
    )
    lane = lax.broadcasted_iota(jnp.int32, (rows, LANES), 1)
    row = lax.broadcasted_iota(jnp.int32, (rows, LANES), 0) % SUB
    reach_of_key = jnp.max(
        jnp.abs(key_buf[:, :HEAD_SIZE].astype(jnp.float32)), axis=0, keepdims=True
    )

    def own(step):
        return slice(step * SUB, (step + 1) * SUB)

    def span(step):
        return slice(step * rows, (step + 1) * rows)

    def window(step):
        return slice(step * SUB, step * SUB + KEYS)

    def tile_steps(tile):
        return max(0, tile - step_tiles + 1), min(steps, tile + 1)

    def limit(step, tile, part):
        place = tile - step
        if 0 < place < step_tiles - 1:
            return part
        halves = []
        for block in range(SUB // BLOCK):
            inside = lane > row % BLOCK if place == 0 else lane <= row % BLOCK
            inside = inside | (row // BLOCK != block)
            halves.append(
                jnp.where(inside, part[:, block * BLOCK : (block + 1) * BLOCK], FORBIDDEN)
            )
        return jnp.concatenate(halves, axis=1)

    for step in range(steps):
        cosines = cos_ref[own(step), :]
        sines = sin_ref[own(step), :]
        adapted = query_ref[own(step), :].astype(jnp.float32) + mm(query_low_ref[own(step), :], query_up)
        turned = []
        for head in range(GROUPS):
            part = adapted[:, head * HEAD_SIZE : (head + 1) * HEAD_SIZE]
            turned.append(part * cosines + swap_halves(part) * sines)
        queries = jnp.concatenate(turned, axis=0) * (SCORE_SCALE * LOG2_E)
        bound = jnp.sum(jnp.abs(queries) * reach_of_key, axis=1, keepdims=True)
        chosen = (lane == row // BLOCK + step * (SUB // BLOCK)).astype(jnp.float32)
        query_buf[span(step), :HEAD_SIZE] = queries.astype(jnp.bfloat16)
        query_buf[span(step), HEAD_SIZE:] = jnp.where(lane == OFFSET_LANE, -bound, chosen).astype(
            jnp.bfloat16
        )
        gradient_buf[span(step), :HEAD_SIZE] = jnp.concatenate(
            [
                gradient_ref[own(step), head * HEAD_SIZE : (head + 1) * HEAD_SIZE]
                for head in range(GROUPS)
            ],
            axis=0,
        )

    def forward():
        for tile in range(tiles):
            low, high = tile_steps(tile)
            cols = slice(tile * SUB, (tile + 1) * SUB)
            scores = mm(query_buf[low * rows : high * rows, :], key_buf[cols, :], BOTH_MINOR)
            for step in range(low, high):
                part = limit(step, tile, scores[(step - low) * rows : (step - low + 1) * rows, :])
                weight_buf[span(step), cols] = jnp.exp2(part).astype(jnp.bfloat16)
        for step in range(steps):
            product_buf[span(step), :] = mm(weight_buf[span(step), window(step)], value_buf[window(step), :])

    forward()
    ones = slice(HEAD_SIZE + ONES_LANE, HEAD_SIZE + ONES_LANE + 1)

    @pl.when(jnp.min(product_buf[:, ones]) < 1e-18)
    def _():
        for step in range(steps):
            extra = query_buf[span(step), HEAD_SIZE:].astype(jnp.float32)
            query_buf[span(step), HEAD_SIZE:] = jnp.where(lane == OFFSET_LANE, 0.0, extra).astype(
                jnp.bfloat16
            )
            highest = jnp.full((rows, 1), FORBIDDEN, jnp.float32)
            for tile in range(step, step + step_tiles):
                cols = slice(tile * SUB, (tile + 1) * SUB)
                part = mm(query_buf[span(step), :], key_buf[cols, :], BOTH_MINOR)
                part = limit(step, tile, part)
                highest = jnp.maximum(highest, jnp.max(part, axis=1, keepdims=True))
            query_buf[span(step), HEAD_SIZE:] = jnp.where(lane == OFFSET_LANE, -highest, extra).astype(
                jnp.bfloat16
            )
        forward()

    spreads = []
    inverses = []
    up_value = jnp.zeros((LANES, HEAD_SIZE), jnp.float32)
    for step in range(steps):
        gradient = gradient_buf[span(step), :HEAD_SIZE]
        gradient_low = mm(gradient, value_up, BOTH_MINOR)
        inverse = 1.0 / product_buf[span(step), ones]
        low_part = (product_buf[span(step), HEAD_SIZE:] * inverse).astype(jnp.bfloat16)
        outputs = product_buf[span(step), :HEAD_SIZE] * inverse + mm(low_part, value_up)
        outputs = outputs.astype(jnp.bfloat16)
        for head in range(GROUPS):
            out_ref[own(step), head * HEAD_SIZE : (head + 1) * HEAD_SIZE] = outputs[own(head), :]
        delta = jnp.sum(
            outputs.astype(jnp.float32) * gradient.astype(jnp.float32), axis=1, keepdims=True
        )
        delta_high = delta.astype(jnp.bfloat16).astype(jnp.float32)
        extra = jnp.where(lane == ONES_LANE, -delta_high, gradient_low)
        extra = jnp.where(lane == ONES_LANE + 1, delta_high - delta, extra)
        gradient_buf[span(step), HEAD_SIZE:] = extra.astype(jnp.bfloat16)
        up_value += mm(low_part, gradient, BOTH_MAJOR)
        spreads.append(jnp.transpose(gradient_low * inverse)[:RANK, :].astype(jnp.bfloat16))
        inverses.append(inverse * SCORE_SCALE)
    up_value_ref[...] = up_value[:RANK, :]
    spread = jnp.concatenate(spreads, axis=1)

    for tile in range(tiles):
        low, high = tile_steps(tile)
        cols = slice(tile * SUB, (tile + 1) * SUB)
        part = slice(low * rows, high * rows)
        grad_weights = mm(gradient_buf[part, :], value_buf[cols, :], BOTH_MINOR)
        weights = weight_buf[part, cols]
        score_buf[part, cols] = weights * grad_weights.astype(jnp.bfloat16)
        value_back_ref[:, cols] += mm(spread[:, part], weights)

    query_grads = []
    for step in range(steps):
        cosines = cos_ref[own(step), :]
        sines = sin_ref[own(step), :]
        sums = mm(score_buf[span(step), window(step)], key_buf[window(step), :HEAD_SIZE]) * inverses[step]
        turned = []
        for head in range(GROUPS):
            part = sums[own(head), :]
            turned.append(part * cosines - swap_halves(part) * sines)
        query_grads.append(jnp.concatenate(turned, axis=1).astype(jnp.bfloat16))
    query_grad = jnp.concatenate(query_grads, axis=0)
    up_query_ref[...] = mm(query_low_t_ref[...], query_grad)
    query_back_ref[...] += mm(query_up, query_grad, BOTH_MINOR)


def attention_chunk(first, last, scalars, query_base, gradient, received, shared, lows, carried):
    count = last - first
    tokens = query_base.shape[0]
    keys = 3 * tokens
    wide = pl.BlockSpec((tokens, GROUP_WIDTH), lambda i, *s: (0, first + i))
    near = pl.BlockSpec((tokens, HEAD_SIZE), lambda i, *s: (0, i))
    far = pl.BlockSpec((tokens, HEAD_SIZE), lambda i, *s: (0, count + i))
    low_rows = pl.BlockSpec((RANK, tokens), lambda i, *s: (tokens // RANK, 0))

    def whole(rows, cols):
        return pl.BlockSpec((rows, cols), lambda i, *s: (0, 0))

    in_specs = [
        wide,
        wide,
        *([near, far] * 4),
        pl.BlockSpec((RANK, GROUP_WIDTH), lambda i, *s: (0, first + i)),
        pl.BlockSpec((RANK, HEAD_SIZE), lambda i, *s: (0, first + i)),
        whole(tokens, RANK),
        whole(RANK, tokens),
        whole(tokens, HEAD_SIZE),
        whole(tokens, HEAD_SIZE),
        *([low_rows] * 4),
    ]
    arguments = [query_base, gradient]
    for array in received:
        arguments += [array, array]
    arguments += [*shared, *lows]
    aliases = {}
    if carried is not None:
        in_specs += [pl.BlockSpec(memory_space=pl.ANY), whole(RANK, tokens), whole(RANK, keys)]
        arguments += list(carried)
        aliases = {len(scalars) + len(arguments) - 3: 0}
    rows = GROUPS * tokens
    wide_buf = HEAD_SIZE + LANES
    return pl.pallas_call(
        functools.partial(attention_kernel, carried is None),
        grid_spec=pltpu.PrefetchScalarGridSpec(
            num_scalar_prefetch=len(scalars),
            grid=(count,),
            in_specs=in_specs,
            out_specs=[
                wide,
                pl.BlockSpec((RANK, GROUP_WIDTH), lambda i, *s: (0, i)),
                pl.BlockSpec((RANK, HEAD_SIZE), lambda i, *s: (0, i)),
                whole(RANK, tokens),
                whole(RANK, keys),
            ],
            scratch_shapes=[
                pltpu.VMEM((keys, wide_buf), jnp.bfloat16),
                pltpu.VMEM((keys, wide_buf), jnp.bfloat16),
                pltpu.VMEM((rows, wide_buf), jnp.bfloat16),
                pltpu.VMEM((rows, wide_buf), jnp.bfloat16),
                pltpu.VMEM((rows, keys), jnp.bfloat16),
                pltpu.VMEM((rows, keys), jnp.bfloat16),
                pltpu.VMEM((rows, wide_buf), jnp.float32),
            ],
        ),
        out_shape=[
            jax.ShapeDtypeStruct(query_base.shape, jnp.bfloat16),
            jax.ShapeDtypeStruct((RANK, count * GROUP_WIDTH), jnp.float32),
            jax.ShapeDtypeStruct((RANK, count * HEAD_SIZE), jnp.float32),
            jax.ShapeDtypeStruct((RANK, tokens), jnp.float32),
            jax.ShapeDtypeStruct((RANK, keys), jnp.float32),
        ],
        input_output_aliases=aliases,
        compiler_params=pltpu.CompilerParams(vmem_limit_bytes=50 * 2**20),
    )(*scalars, *arguments)


def head_sum(x):
    if lax.axis_size("head") == 2:
        return x + lax.ppermute(x, "head", [(0, 1), (1, 0)])
    return lax.psum(x, "head")


def after(value, *others):
    return lax.optimization_barrier((value, *others))[0]


def per_device(
    hidden_states,
    query_base,
    key_base,
    frozen_value_rows,
    query_down,
    query_up,
    value_down,
    value_up_weight,
    positions,
    block_mask,
    output_gradient,
):
    tokens = hidden_states.shape[0]
    devices = lax.axis_size("ctx")
    device_index = lax.axis_index("ctx")
    kv_heads = key_base.shape[1] // HEAD_SIZE
    forward_one = [(i, i + 1) for i in range(devices - 1)]
    even_two = [(i, i + 2) for i in range(0, devices - 2, 2)]
    even_one = [(i, i + 1) for i in range(0, devices - 1, 2)]

    both_down = jnp.concatenate([query_down, value_down], axis=1)
    low = head_sum(mm(both_down, hidden_states, (((0,), (1,)), ((), ())))).astype(jnp.bfloat16)
    query_low_t = low[:RANK]
    value_low_t = low[RANK:]

    half = np.arange(HEAD_SIZE // 2, dtype=np.float64)
    frequency = (ROPE_BASE ** (-2.0 * half / HEAD_SIZE)).astype(np.float32)[:, None]
    cosines, sines, *packed = pl.pallas_call(
        functools.partial(prologue_kernel, CHUNKS),
        out_shape=[
            jax.ShapeDtypeStruct((tokens, HEAD_SIZE), jnp.float32),
            jax.ShapeDtypeStruct((tokens, HEAD_SIZE), jnp.float32),
            *(
                jax.ShapeDtypeStruct(
                    (tokens + (RANK if first == 0 else 0), 2 * (last - first) * HEAD_SIZE),
                    jnp.bfloat16,
                )
                for first, last in CHUNKS
            ),
        ],
        compiler_params=pltpu.CompilerParams(vmem_limit_bytes=50 * 2**20),
    )(positions[None, :], jnp.asarray(frequency), key_base, frozen_value_rows)
    packed[0] = lax.dynamic_update_slice(packed[0], value_low_t, (tokens, 0))

    place = jnp.stack([device_index, device_index % 2]).astype(jnp.int32)
    scalars = (place, block_mask.T)
    shared = (query_up, value_up_weight, query_low_t.T, query_low_t, cosines, sines)

    ones, evens = [], []
    for chunk, own in enumerate(packed):
        if chunk == 1:
            own = after(own, ones[0])
        elif chunk == 2:
            own = after(own, evens[0])
        elif chunk > 2:
            own = after(own, ones[chunk - 2], evens[chunk - 2])
        ones.append(lax.ppermute(own, "ctx", forward_one))
        evens.append(lax.ppermute(own, "ctx", even_two))

    carried = None
    lows = None
    up_queries, up_values = [], []
    for chunk, (first, last) in enumerate(CHUNKS):
        one = ones[chunk]
        if carried is not None:
            one = after(one, carried[1])
        odd = lax.ppermute(one, "ctx", even_one)
        received = (packed[chunk], one, evens[chunk], odd)
        if lows is None:
            lows = received
        attention_out, up_query, up_value, query_back, value_back = attention_chunk(
            first,
            last,
            scalars,
            query_base,
            output_gradient,
            received,
            shared,
            lows,
            carried,
        )
        carried = (attention_out, query_back, value_back)
        up_queries.append(up_query)
        up_values.append(up_value)

    back_one = lax.ppermute(
        value_back[:, tokens : 2 * tokens], "ctx", [(i + 1, i) for i in range(devices - 1)]
    )
    back_two = lax.ppermute(value_back[:, :tokens], "ctx", [(i + 2, i) for i in range(devices - 2)])
    value_back = value_back[:, 2 * tokens :] + back_one + back_two
    back = head_sum(jnp.concatenate([query_back, value_back], axis=0)).astype(jnp.bfloat16)
    down = mm(back, hidden_states)
    features = down.shape[1]
    partial = jnp.concatenate([down[:RANK], down[RANK:], *up_queries, *up_values], axis=1)
    columns = partial.shape[1]
    piece = -(-columns // (devices * LANES)) * LANES
    partial = jnp.pad(partial.astype(jnp.bfloat16), ((0, 0), (0, devices * piece - columns)))
    partial = partial.reshape(RANK, devices, piece).transpose(1, 0, 2)
    received = lax.all_to_all(partial, "ctx", 0, 0)
    mine = jnp.sum(received.astype(jnp.float32), axis=0) * ((devices * tokens) ** (-0.5))
    mine = jnp.broadcast_to(mine.astype(jnp.bfloat16)[None], (devices, RANK, piece))
    summed = lax.all_to_all(mine, "ctx", 0, 0)
    summed = summed.transpose(1, 0, 2).reshape(RANK, devices * piece).astype(jnp.float32)
    query_columns = kv_heads * GROUP_WIDTH
    up_first = 2 * features
    return (
        attention_out,
        summed[:, :features].T,
        summed[:, up_first : up_first + query_columns],
        summed[:, features:up_first].T,
        summed[:, up_first + query_columns : columns],
    )


def solution(mesh):
    placed = (
        P("ctx", "head"),
        P("ctx", "head"),
        P("ctx", "head"),
        P("ctx", "head"),
        P("head", None),
        P(None, "head"),
        P("head", None),
        P(None, "head"),
        P("ctx"),
        P(),
        P("ctx", "head"),
    )
    return jax.shard_map(
        per_device,
        mesh=mesh,
        in_specs=placed,
        out_specs=(
            P("ctx", "head"),
            P("head", None),
            P(None, "head"),
            P("head", None),
            P(None, "head"),
        ),
        check_vma=False,
    )
```

time: 190 us -> 182 us (0.958)
  Pallas kernels: 67 us -> 78.7 us
  starting transfers between devices: 52 us -> 43 us
  other arithmetic: 6.87 us -> 0.82 us
  local copies, waits for them, and re-layouts: 18.8 us -> 13.9 us
    pallas_call x3 -> x4, Pallas kernels: 63.1 us -> 75.2 us  [attention_chunk(): pl.pallas_call(functools.partial(attention_kernel, carried is None), grid...]
    ppermute x5 -> x4, starting transfers between devices: 23.2 us -> 14.1 us  [per_device(): odd = lax.ppermute(one, 'ctx', even_one)]
    concatenate x3 -> x0, local copies, waits for them, and re-layouts: 2.88 us -> none  [the longest x1 1.72 us: per_device(): value_low = jnp.concatenate([low_two, low_one, value_low_t], axis=1)]
    ppermute x3 -> x4, starting transfers between devices: 8.66 us -> 6.21 us  [per_device(): ones.append(lax.ppermute(own, 'ctx', forward_one))]
    broadcast_in_dim x3 -> x0, local copies, waits for them, and re-layouts: 2.42 us -> none  [the longest x1 1.69 us: per_device(): positions[:, None]]
    ppermute x3 -> x4, starting transfers between devices: 14.6 us -> 16.5 us  [per_device(): evens.append(lax.ppermute(own, 'ctx', even_two))]
    unnamed x33 -> x44, local copies, waits for them, and re-layouts: 8 us -> 9.63 us
  transfers between devices with their start and end apart: 15 -> 16, of which waited for: 5 -> 4; matrix products, arithmetic and copies ran while one was open for 9% -> 1% of each run, Pallas kernels for 25% -> 33%
where the time goes in v2:
time: 182 us; the launch traced here: 181 us
  Pallas kernels  78.7 us (43%)
  starting transfers between devices  43 us (24%)
  blocking collectives  30.8 us (17%)
  local copies, waits for them, and re-layouts  13.9 us (8%)
  waiting for transfers between devices  10.6 us (6%)
  matrix products  2.39 us (1%)
    pallas_call x4, Pallas kernels, attention_chunk(): pl.pallas_call(functools.partial(attention_kernel, carried is None), grid...  75.2 us
    all_to_all x1, blocking collectives, per_device(): received = lax.all_to_all(partial, 'ctx', 0, 0)  16.6 us
    ppermute x4, starting transfers between devices, per_device(): evens.append(lax.ppermute(own, 'ctx', even_two))  16.5 us
    all_to_all x1, blocking collectives, per_device(): summed = lax.all_to_all(mine, 'ctx', 0, 0)  14.1 us
    ppermute x4, starting transfers between devices, per_device(): odd = lax.ppermute(one, 'ctx', even_one)  14.1 us
    unnamed x44, local copies, waits for them, and re-layouts  9.63 us
    ppermute x4, starting transfers between devices, per_device(): ones.append(lax.ppermute(own, 'ctx', forward_one))  6.21 us
    ppermute x1, waiting for transfers between devices, per_device(): lax.ppermute(value_back[:, :tokens], 'ctx', [(i + 2, i) for i in range(de...  5.17 us
  transfers between devices with their start and end apart: 16, of which 4 were waited for; matrix products, arithmetic and copies ran while one was open for 1% of the time, Pallas kernels for 33%

profile of v2, /device:TPU:0, one launch (start us, length us, event | category | flops | bytes accessed | tf_op | source)
XLA Modules:
  0.0 181.3 jit_solution(13912064087942314052)
XLA Ops:
  0.7 1.7 copy-done
  2.4 1.8 %fusion = f32[32,512]{1,0:T(8,128)S(1)} fusion(bf16[512,2688]{1,0:T(8,128)(2,1)S(1)} %copy-done, bf16[2688,16]{0,1:T(8,128)(2,1)} %param.18, bf16[2688,16]{0,1:T(8,128)(2,1)} %param.16), kind=kOutput, calls=%fused_computation.6 | convolution fusion | flops 88424448 | bytes 2990080 | tf_op jit(solution)/shard_map/dot_general | solution.py:39
  4.2 3.0 %collective-permute-start = (f32[32,512]{1,0:T(8,128)S(1)}, f32[32,512]{1,0:T(8,128)S(1)}, u32[]{:S(2)}, u32[]{:S(2)}) collective-permute-start(f32[32,512]{1,0:T(8,128)S(1)} %fusion), channel_id=1, source_target_pairs={{0,1},{1,0},{2,3},{3,2},{4,5},{5,4},{6,7},{7,6},{8,9},{9,8},{10,11... | collective-permute-start | bytes 196616 | tf_op jit(solution)/shard_map/ppermute | solution.py:360
  7.2 3.5 %shard_map.155 = (f32[512,128]{1,0:T(8,128)S(1)}, f32[512,128]{1,0:T(8,128)S(1)}, bf16[528,512]{1,0:T(8,128)(2,1)}, bf16[512,512]{1,0:T(8,128)(2,1)}, bf16[512,5...) custom-call(s32[1,512]{1,0:T(1,128)S(1)} %bitcast.27, f32[64,1]{1,0:T(8,128)S(1)} %copy-done.18, ...), custom_call_target="tpu_custom_call" | custom-call | tf_op jit(solution)/shard_map/pallas_call | solution.py:396
  11.4 0.8 copy-done.6
  13.6 1.5 collective-permute-start.1
  15.1 4.7 %collective-permute-start.5 = (bf16[528,512]{1,0:T(8,128)(2,1)}, bf16[528,512]{1,0:T(8,128)(2,1)}, u32[]{:S(2)}, u32[]{:S(2)}) collective-permute-start(bf16[528,512]{1,0:T(8,128)(2,1)} %get-tuple-element.75.key_own_ref.value_own_ref.low_own_ref), channel_id=1, source_target_pairs={{0,4},{4,8},{8,12},{12,16},{16,20},{20,24},{24,28},{1,5},{5,9},{9,... | collective-permute-start | bytes 1622024 | tf_op jit(solution)/shard_map/ppermute | solution.py:426
  19.8 9.9 %collective-permute-start.7 = (bf16[528,512]{1,0:T(8,128)(2,1)S(1)}, bf16[528,512]{1,0:T(8,128)(2,1)}, u32[]{:S(2)}, u32[]{:S(2)}) collective-permute-start(bf16[528,512]{1,0:T(8,128)(2,1)S(1)} %collective-permute-done.1.key_one_ref.value_one_ref.low_one_ref), channel_id=1, source_target_pairs={{0,2},{4,6},{8,10},{12,14},{16,18},{20,22},{24,26},{28,30},{1,3},{... | collective-permute-start | bytes 1622024 | tf_op jit(solution)/shard_map/ppermute | solution.py:435
  29.7 2.1 %collective-permute-start.2 = (bf16[512,512]{1,0:T(8,128)(2,1)}, bf16[512,512]{1,0:T(8,128)(2,1)}, u32[]{:S(2)}, u32[]{:S(2)}) collective-permute-start(bf16[512,512]{1,0:T(8,128)(2,1)} %get-tuple-element.40.key_own_ref.value_own_ref), channel_id=1, source_target_pairs={{0,2},{2,4},{4,6},{6,8},{8,10},{10,12},{12,14},{14,16},{16,18},{18... | collective-permute-start | bytes 1572872 | tf_op jit(solution)/shard_map/ppermute | solution.py:425
  32.4 1.5 copy.29.query_low_ref
  33.9 3.4 %collective-permute-start.3 = (bf16[512,512]{1,0:T(8,128)(2,1)}, bf16[512,512]{1,0:T(8,128)(2,1)S(1)}, u32[]{:S(2)}, u32[]{:S(2)}) collective-permute-start(bf16[512,512]{1,0:T(8,128)(2,1)} %get-tuple-element.40.key_own_ref.value_own_ref), channel_id=1, source_target_pairs={{0,4},{4,8},{8,12},{12,16},{16,20},{20,24},{24,28},{1,5},{5,9},{9,... | collective-permute-start | bytes 1572872 | tf_op jit(solution)/shard_map/ppermute | solution.py:426
  37.3 0.9 copy-done.3
  38.3 0.9 copy-done.4
  39.2 0.8 copy-done.10
  42.9 19.0 %shard_map.156 = (bf16[512,2048]{1,0:T(8,128)(2,1)}, f32[16,512]{1,0:T(8,128)S(1)}, f32[16,256]{1,0:T(8,128)S(1)}, f32[16,512]{1,0:T(8,128)S(1)}, f32[16,1536]{1,0:T(8,128)S(1)}) custom-call(s32[2]{0:T(128)S(1)} %copy-done.19, s32[9,64]{1,0:T(8,128)S(1)} %bitcast.23, bf16[512,2048]{1,0:T(8,128)(2,1)} %query_ref.7, bf16[512,2048]{1,0:T(8,128)(2,1)} %gradient_ref.7, ...), custom_call_target="tpu_custom_call" | custom-call | tf_op jit(solution)/shard_map/pallas_call | solution.py:323
  61.9 1.3 collective-permute-start.8
  63.2 1.3 collective-permute-start.6
  64.5 5.1 %collective-permute-start.9 = (bf16[512,512]{1,0:T(8,128)(2,1)S(1)}, bf16[512,512]{1,0:T(8,128)(2,1)S(1)}, u32[]{:S(2)}, u32[]{:S(2)}) collective-permute-start(bf16[512,512]{1,0:T(8,128)(2,1)S(1)} %copy-done.9), channel_id=1, source_target_pairs={{0,4},{4,8},{8,12},{12,16},{16,20},{20,24},{24,28},{1,5},{5,9},{9,... | collective-permute-start | bytes 1572872 | tf_op jit(solution)/shard_map/ppermute | solution.py:426
  69.7 18.9 %shard_map.157 = (bf16[512,2048]{1,0:T(8,128)(2,1)}, f32[16,512]{1,0:T(8,128)S(1)}, f32[16,256]{1,0:T(8,128)S(1)}, f32[16,512]{1,0:T(8,128)S(1)}, f32[16,1536]{1,0:T(8,128)S(1)}) custom-call(s32[2]{0:T(128)S(1)} %copy-done.19, s32[9,64]{1,0:T(8,128)S(1)} %bitcast.24, bf16[512,2048]{1,0:T(8,128)(2,1)} %query_ref.7, ...), custom_call_target="tpu_custom_call", output_to_operand_aliasing={{0}: (22, {})} | custom-call | tf_op jit(solution)/shard_map/pallas_call | solution.py:323
  88.6 1.3 collective-permute-start.10
  90.0 1.3 collective-permute-start.4
  91.3 3.3 %collective-permute-start.11 = (bf16[512,512]{1,0:T(8,128)(2,1)S(1)}, bf16[512,512]{1,0:T(8,128)(2,1)S(1)}, u32[]{:S(2)}, u32[]{:S(2)}) collective-permute-start(bf16[512,512]{1,0:T(8,128)(2,1)S(1)} %copy-done.7), channel_id=1, source_target_pairs={{0,4},{4,8},{8,12},{12,16},{16,20},{20,24},{24,28},{1,5},{5,9},{9,... | collective-permute-start | bytes 1572872 | tf_op jit(solution)/shard_map/ppermute | solution.py:426
  94.7 18.7 %shard_map.158 = (bf16[512,2048]{1,0:T(8,128)(2,1)}, f32[16,512]{1,0:T(8,128)S(1)}, f32[16,256]{1,0:T(8,128)S(1)}, f32[16,512]{1,0:T(8,128)S(1)}, f32[16,1536]{1,0:T(8,128)S(1)}) custom-call(s32[2]{0:T(128)S(1)} %copy-done.19, s32[9,64]{1,0:T(8,128)S(1)} %bitcast.25, bf16[512,2048]{1,0:T(8,128)(2,1)} %query_ref.7, ...), custom_call_target="tpu_custom_call", output_to_operand_aliasing={{0}: (22, {})} | custom-call | tf_op jit(solution)/shard_map/pallas_call | solution.py:323
  113.4 1.6 collective-permute-start.12
  115.0 1.2 collective-permute-done.12.key_odd_ref.value_odd_ref
  116.2 18.7 %shard_map.159 = (bf16[512,2048]{1,0:T(8,128)(2,1)}, f32[16,512]{1,0:T(8,128)S(1)}, f32[16,256]{1,0:T(8,128)S(1)}, f32[16,512]{1,0:T(8,128)S(1)}, f32[16,1536]{1,0:T(8,128)S(1)}) custom-call(s32[2]{0:T(128)S(1)} %copy-done.19, s32[9,64]{1,0:T(8,128)S(1)} %bitcast.26, bf16[512,2048]{1,0:T(8,128)(2,1)} %query_ref.7, ...), custom_call_target="tpu_custom_call", output_to_operand_aliasing={{0}: (22, {})} | custom-call | tf_op jit(solution)/shard_map/pallas_call | solution.py:323
  134.8 1.3 collective-permute-start.13
  136.1 1.3 collective-permute-start.14
  137.9 5.2 %collective-permute-done.14 = f32[16,512]{1,0:T(8,128)S(1)} collective-permute-done((f32[16,512]{1,0:T(8,128)S(1)}, f32[16,512]{1,0:T(8,128)S(1)}, u32[]{:S(2)}, u32[]{:S(2)}) %collective-permute-start.14) | collective-permute-done | bytes 32800 | tf_op jit(solution)/shard_map/ppermute | solution.py:457
  143.7 3.7 %collective-permute-done.15 = f32[32,512]{1,0:T(8,128)S(1)} collective-permute-done((f32[32,512]{1,0:T(8,128)S(1)}, f32[32,512]{1,0:T(8,128)S(1)}, u32[]{:S(2)}, u32[]{:S(2)}) %collective-permute-start.15) | collective-permute-done | bytes 65568 | tf_op jit(solution)/shard_map/ppermute | solution.py:360
  148.3 16.6 %all_to_all.10 = bf16[16,16,640]{2,1,0:T(8,128)(2,1)S(1)} all-to-all(bf16[16,16,640]{2,1,0:T(8,128)(2,1)S(1)} %bitcast.32), channel_id=1, replica_groups=mesh['ctx'=16,'head'=2] {'ctx'}, dimensions={0} | all-to-all | bytes 655360 | tf_op jit(solution)/shard_map/all_to_all | solution.py:467
  165.0 14.1 %all_to_all.11 = bf16[16,16,640]{2,1,0:T(8,128)(2,1)S(1)} all-to-all(bf16[16,16,640]{2,1,0:T(8,128)(2,1)S(1)} %broadcast_in_dim.10), channel_id=1, replica_groups=mesh['ctx'=16,'head'=2] {'ctx'}, dimensions={0} | all-to-all | bytes 655360 | tf_op jit(solution)/shard_map/all_to_all | solution.py:470
  (78 shorter events, 9.7 us)
Async XLA Ops:
  0.6 1.8 copy-start
  0.6 6.6 %copy-start.18 = (f32[64,1]{1,0:T(8,128)S(1)}, f32[64,1]{1,0:T(8,128)}, u32[]{:S(2)}) copy-start(f32[64,1]{1,0:T(8,128)} %constant.30.clone.frequency_ref) | copy-start | bytes 772
  0.7 6.5 %copy-start.20 = (s32[512]{0:T(512)S(1)}, s32[512]{0:T(512)}, u32[]{:S(2)}) copy-start(s32[512]{0:T(512)} %param.20) | copy-start | bytes 6148
  0.7 6.5 %copy-start.12 = (bf16[512,1024]{1,0:T(8,128)(2,1)S(1)}, bf16[512,1024]{1,0:T(8,128)(2,1)}, u32[]{:S(2)}) copy-start(bf16[512,1024]{1,0:T(8,128)(2,1)} %key_ref.1) | copy-start | bytes 3145732
  4.2 8.7 %collective-permute-start = (f32[32,512]{1,0:T(8,128)S(1)}, f32[32,512]{1,0:T(8,128)S(1)}, u32[]{:S(2)}, u32[]{:S(2)}) collective-permute-start(f32[32,512]{1,0:T(8,128)S(1)} %fusion), channel_id=1, source_target_pairs={{0,1},{1,0},{2,3},{3,2},{4,5},{5,4},{6,7},{7,6},{8,9},{9,8},{10,11... | collective-permute-start | bytes 196616 | tf_op jit(solution)/shard_map/ppermute | solution.py:360
  11.4 0.8 copy-start.6
  12.2 0.8 copy-start.8
  13.6 6.2 %collective-permute-start.1 = (bf16[528,512]{1,0:T(8,128)(2,1)}, bf16[528,512]{1,0:T(8,128)(2,1)S(1)}, u32[]{:S(2)}, u32[]{:S(2)}) collective-permute-start(bf16[528,512]{1,0:T(8,128)(2,1)} %get-tuple-element.75.key_own_ref.value_own_ref.low_own_ref), channel_id=1, source_target_pairs={{0,2},{2,4},{4,6},{6,8},{8,10},{10,12},{12,14},{14,16},{16,18},{18... | collective-permute-start | bytes 1622024 | tf_op jit(solution)/shard_map/ppermute | solution.py:425
  15.1 22.2 %collective-permute-start.5 = (bf16[528,512]{1,0:T(8,128)(2,1)}, bf16[528,512]{1,0:T(8,128)(2,1)}, u32[]{:S(2)}, u32[]{:S(2)}) collective-permute-start(bf16[528,512]{1,0:T(8,128)(2,1)} %get-tuple-element.75.key_own_ref.value_own_ref.low_own_ref), channel_id=1, source_target_pairs={{0,4},{4,8},{8,12},{12,16},{16,20},{20,24},{24,28},{1,5},{5,9},{9,... | collective-permute-start | bytes 1622024 | tf_op jit(solution)/shard_map/ppermute | solution.py:426
  19.8 42.1 %copy-start.1 = (bf16[528,512]{1,0:T(8,128)(2,1)}, bf16[528,512]{1,0:T(8,128)(2,1)S(1)}, u32[]{:S(2)}) copy-start(bf16[528,512]{1,0:T(8,128)(2,1)S(1)} %collective-permute-done.1.key_one_ref.value_one_ref.low_one_ref) | copy-start | bytes 1622020
  19.8 17.5 %collective-permute-start.7 = (bf16[528,512]{1,0:T(8,128)(2,1)S(1)}, bf16[528,512]{1,0:T(8,128)(2,1)}, u32[]{:S(2)}, u32[]{:S(2)}) collective-permute-start(bf16[528,512]{1,0:T(8,128)(2,1)S(1)} %collective-permute-done.1.key_one_ref.value_one_ref.low_one_ref), channel_id=1, source_target_pairs={{0,2},{4,6},{8,10},{12,14},{16,18},{20,22},{24,26},{28,30},{1,3},{... | collective-permute-start | bytes 1622024 | tf_op jit(solution)/shard_map/ppermute | solution.py:435
  29.7 32.2 %collective-permute-start.2 = (bf16[512,512]{1,0:T(8,128)(2,1)}, bf16[512,512]{1,0:T(8,128)(2,1)}, u32[]{:S(2)}, u32[]{:S(2)}) collective-permute-start(bf16[512,512]{1,0:T(8,128)(2,1)} %get-tuple-element.40.key_own_ref.value_own_ref), channel_id=1, source_target_pairs={{0,2},{2,4},{4,6},{6,8},{8,10},{10,12},{12,14},{14,16},{16,18},{18... | collective-permute-start | bytes 1572872 | tf_op jit(solution)/shard_map/ppermute | solution.py:425
  33.9 35.8 %collective-permute-start.3 = (bf16[512,512]{1,0:T(8,128)(2,1)}, bf16[512,512]{1,0:T(8,128)(2,1)S(1)}, u32[]{:S(2)}, u32[]{:S(2)}) collective-permute-start(bf16[512,512]{1,0:T(8,128)(2,1)} %get-tuple-element.40.key_own_ref.value_own_ref), channel_id=1, source_target_pairs={{0,4},{4,8},{8,12},{12,16},{16,20},{20,24},{24,28},{1,5},{5,9},{9,... | collective-permute-start | bytes 1572872 | tf_op jit(solution)/shard_map/ppermute | solution.py:426
  37.3 1.0 copy-start.3
  38.3 0.9 copy-start.4
  39.2 0.8 copy-start.10
  42.9 20.4 %copy-start.9 = (bf16[512,512]{1,0:T(8,128)(2,1)S(1)}, bf16[512,512]{1,0:T(8,128)(2,1)}, u32[]{:S(2)}) copy-start(bf16[512,512]{1,0:T(8,128)(2,1)} %copy-done.8) | copy-start | bytes 1572868
  42.9 26.8 %copy-start.5 = (bf16[512,16]{1,0:T(8,128)(2,1)S(1)}, bf16[512,16]{1,0:T(8,128)(2,1)}, u32[]{:S(2)}) copy-start(bf16[512,16]{1,0:T(8,128)(2,1)} %copy.29.query_low_ref) | copy-start | bytes 49156
  42.9 26.8 %copy-start.11 = (bf16[16,2048]{1,0:T(8,128)(2,1)S(1)}, bf16[16,2048]{1,0:T(8,128)(2,1)}, u32[]{:S(2)}) copy-start(bf16[16,2048]{1,0:T(8,128)(2,1)} %query_up_ref.7) | copy-start | bytes 196612
  42.9 26.8 %copy-start.14 = (bf16[16,1024]{1,0:T(8,128)(2,1)S(1)}, bf16[16,1024]{1,0:T(8,128)(2,1)}, u32[]{:S(2)}) copy-start(bf16[16,1024]{1,0:T(8,128)(2,1)} %value_up_ref.7) | copy-start | bytes 98308
  42.9 26.8 %copy-start.16 = (bf16[16,512]{1,0:T(8,128)(2,1)S(1)}, bf16[16,512]{1,0:T(8,128)(2,1)}, u32[]{:S(2)}) copy-start(bf16[16,512]{1,0:T(8,128)(2,1)} %get-tuple-element.73.query_low_t_ref) | copy-start | bytes 49156
  61.9 7.8 %collective-permute-start.8 = (bf16[512,512]{1,0:T(8,128)(2,1)}, bf16[512,512]{1,0:T(8,128)(2,1)S(1)}, u32[]{:S(2)}, u32[]{:S(2)}) collective-permute-start(bf16[512,512]{1,0:T(8,128)(2,1)} %collective-permute-done.2.key_one_ref.value_one_ref), channel_id=1, source_target_pairs={{0,2},{4,6},{8,10},{12,14},{16,18},{20,22},{24,26},{28,30},{1,3},{... | collective-permute-start | bytes 1572872 | tf_op jit(solution)/shard_map/ppermute | solution.py:435
  63.2 25.4 %collective-permute-start.6 = (bf16[512,512]{1,0:T(8,128)(2,1)S(1)}, bf16[512,512]{1,0:T(8,128)(2,1)S(1)}, u32[]{:S(2)}, u32[]{:S(2)}) collective-permute-start(bf16[512,512]{1,0:T(8,128)(2,1)S(1)} %copy-done.9), channel_id=1, source_target_pairs={{0,2},{2,4},{4,6},{6,8},{8,10},{10,12},{12,14},{14,16},{16,18},{18... | collective-permute-start | bytes 1572872 | tf_op jit(solution)/shard_map/ppermute | solution.py:425
  64.5 30.1 %collective-permute-start.9 = (bf16[512,512]{1,0:T(8,128)(2,1)S(1)}, bf16[512,512]{1,0:T(8,128)(2,1)S(1)}, u32[]{:S(2)}, u32[]{:S(2)}) collective-permute-start(bf16[512,512]{1,0:T(8,128)(2,1)S(1)} %copy-done.9), channel_id=1, source_target_pairs={{0,4},{4,8},{8,12},{12,16},{16,20},{20,24},{24,28},{1,5},{5,9},{9,... | collective-permute-start | bytes 1572872 | tf_op jit(solution)/shard_map/ppermute | solution.py:426
  69.7 20.2 %copy-start.7 = (bf16[512,512]{1,0:T(8,128)(2,1)S(1)}, bf16[512,512]{1,0:T(8,128)(2,1)}, u32[]{:S(2)}) copy-start(bf16[512,512]{1,0:T(8,128)(2,1)} %copy-done.6) | copy-start | bytes 1572868
  88.6 6.0 %collective-permute-start.10 = (bf16[512,512]{1,0:T(8,128)(2,1)S(1)}, bf16[512,512]{1,0:T(8,128)(2,1)S(1)}, u32[]{:S(2)}, u32[]{:S(2)}) collective-permute-start(bf16[512,512]{1,0:T(8,128)(2,1)S(1)} %collective-permute-done.6.key_one_ref.value_one_ref), channel_id=1, source_target_pairs={{0,2},{4,6},{8,10},{12,14},{16,18},{20,22},{24,26},{28,30},{1,3},{... | collective-permute-start | bytes 1572872 | tf_op jit(solution)/shard_map/ppermute | solution.py:435
  90.0 23.4 %collective-permute-start.4 = (bf16[512,512]{1,0:T(8,128)(2,1)S(1)}, bf16[512,512]{1,0:T(8,128)(2,1)S(1)}, u32[]{:S(2)}, u32[]{:S(2)}) collective-permute-start(bf16[512,512]{1,0:T(8,128)(2,1)S(1)} %copy-done.7), channel_id=1, source_target_pairs={{0,2},{2,4},{4,6},{6,8},{8,10},{10,12},{12,14},{14,16},{16,18},{18... | collective-permute-start | bytes 1572872 | tf_op jit(solution)/shard_map/ppermute | solution.py:425
  91.3 23.7 %collective-permute-start.11 = (bf16[512,512]{1,0:T(8,128)(2,1)S(1)}, bf16[512,512]{1,0:T(8,128)(2,1)S(1)}, u32[]{:S(2)}, u32[]{:S(2)}) collective-permute-start(bf16[512,512]{1,0:T(8,128)(2,1)S(1)} %copy-done.7), channel_id=1, source_target_pairs={{0,4},{4,8},{8,12},{12,16},{16,20},{20,24},{24,28},{1,5},{5,9},{9,... | collective-permute-start | bytes 1572872 | tf_op jit(solution)/shard_map/ppermute | solution.py:426
  113.4 2.8 %collective-permute-start.12 = (bf16[512,512]{1,0:T(8,128)(2,1)S(1)}, bf16[512,512]{1,0:T(8,128)(2,1)S(1)}, u32[]{:S(2)}, u32[]{:S(2)}) collective-permute-start(bf16[512,512]{1,0:T(8,128)(2,1)S(1)} %collective-permute-done.4.key_one_ref.value_one_ref), channel_id=1, source_target_pairs={{0,2},{4,6},{8,10},{12,14},{16,18},{20,22},{24,26},{28,30},{1,3},{... | collective-permute-start | bytes 1572872 | tf_op jit(solution)/shard_map/ppermute | solution.py:435
  134.8 3.1 %collective-permute-start.13 = (f32[16,512]{1,0:T(8,128)S(1)}, f32[16,512]{1,0:T(8,128)S(1)}, u32[]{:S(2)}, u32[]{:S(2)}) collective-permute-start(f32[16,512]{1,0:T(8,128)S(1)} %get-tuple-element.71), channel_id=1, source_target_pairs={{2,0},{4,2},{6,4},{8,6},{10,8},{12,10},{14,12},{16,14},{18,16},{20... | collective-permute-start | bytes 98312 | tf_op jit(solution)/shard_map/ppermute | solution.py:454
  136.1 7.0 %collective-permute-start.14 = (f32[16,512]{1,0:T(8,128)S(1)}, f32[16,512]{1,0:T(8,128)S(1)}, u32[]{:S(2)}, u32[]{:S(2)}) collective-permute-start(f32[16,512]{1,0:T(8,128)S(1)} %get-tuple-element.72), channel_id=1, source_target_pairs={{4,0},{6,2},{8,4},{10,6},{12,8},{14,10},{16,12},{18,14},{20,16},{2... | collective-permute-start | bytes 98312 | tf_op jit(solution)/shard_map/ppermute | solution.py:457
  143.1 4.3 %collective-permute-start.15 = (f32[32,512]{1,0:T(8,128)S(1)}, f32[32,512]{1,0:T(8,128)S(1)}, u32[]{:S(2)}, u32[]{:S(2)}) collective-permute-start(f32[32,512]{1,0:T(8,128)S(1)} %pad_maximum_fusion), channel_id=1, source_target_pairs={{0,1},{1,0},{2,3},{3,2},{4,5},{5,4},{6,7},{7,6},{8,9},{9,8},{10,11... | collective-permute-start | bytes 196616 | tf_op jit(solution)/shard_map/ppermute | solution.py:360
  (5 other events, 3.5 us)

commit v3 on v2

v3 whole, which is shorter than its diff:
```python
import functools

import jax
import jax.numpy as jnp
import numpy as np
from jax import lax
from jax.experimental import pallas as pl
from jax.experimental.pallas import tpu as pltpu
from jax.sharding import PartitionSpec as P

D = 5376
QUERY_HEADS = 32
KEY_VALUE_HEADS = 16
HEAD_SIZE = 128
WINDOW = 1024
BLOCK = 128
GROUPS = QUERY_HEADS // KEY_VALUE_HEADS
GROUP_WIDTH = GROUPS * HEAD_SIZE
SCORE_SCALE = (D // QUERY_HEADS) ** (-0.5)
LOG2_E = 1.4426950408889634
ROPE_BASE = 10000.0
FORBIDDEN = -1e30
RANK = 16

SUB = 256
KEYS = SUB + WINDOW
LANES = 128
OFFSET_LANE = 64
ONES_LANE = RANK

CHUNKS = ((0, 2), (2, 5), (5, 8))

ROWS_BY_COLS = (((1,), (0,)), ((), ()))
BOTH_MINOR = (((1,), (1,)), ((), ()))
BOTH_MAJOR = (((0,), (0,)), ((), ()))


def mm(left, right, dims=ROWS_BY_COLS):
    return lax.dot_general(left, right, dims, preferred_element_type=jnp.float32)


def swap_halves(x):
    return pltpu.roll(x, HEAD_SIZE // 2, 1)


def prologue_kernel(chunks, positions_ref, frequency_ref, key_ref, value_ref, cos_ref, sin_ref, *outs):
    tokens = key_ref.shape[0]
    half = HEAD_SIZE // 2
    angles = frequency_ref[...] * positions_ref[...].astype(jnp.float32)
    both = jnp.transpose(jnp.concatenate([jnp.cos(angles), jnp.sin(angles)], axis=0))
    turned = swap_halves(both)
    low_half = lax.broadcasted_iota(jnp.int32, both.shape, 1) < half
    cosines = jnp.where(low_half, both, turned)
    sines = jnp.where(low_half, -turned, both)
    cos_ref[...] = cosines
    sin_ref[...] = sines
    own = pl.ds(0, tokens)
    for (first, last), out_ref in zip(chunks, outs):
        count = last - first
        for head in range(first, last):
            cols = pl.ds(head * HEAD_SIZE, HEAD_SIZE)
            key = key_ref[:, cols].astype(jnp.float32)
            rotated = key * cosines + swap_halves(key) * sines
            out_ref[own, pl.ds((head - first) * HEAD_SIZE, HEAD_SIZE)] = rotated.astype(jnp.bfloat16)
            out_ref[own, pl.ds((count + head - first) * HEAD_SIZE, HEAD_SIZE)] = value_ref[:, cols]


def attention_kernel(first, place_ref, *refs):
    if first:
        mask_ref, *refs = refs
    (
        query_ref,
        gradient_ref,
        key_own_ref,
        value_own_ref,
        key_one_ref,
        value_one_ref,
        key_even_ref,
        value_even_ref,
        key_odd_ref,
        value_odd_ref,
        query_up_ref,
        value_up_ref,
        query_low_ref,
        query_low_t_ref,
        cos_ref,
        sin_ref,
        *refs,
    ) = refs
    if first:
        low_own_ref, low_one_ref, low_even_ref, low_odd_ref, *refs = refs
    else:
        key_extra_in, value_extra_in, _, query_back_in, value_back_in, *refs = refs
    out_ref, up_query_ref, up_value_ref, query_back_ref, value_back_ref, *refs = refs
    if first:
        key_extra_ref, value_extra_ref, *refs = refs
    key_buf, value_buf, query_buf, gradient_buf, weight_buf, score_buf, product_buf = refs
    steps = query_back_ref.shape[0]
    tokens = steps * SUB
    keys = key_buf.shape[0]
    step_tiles = KEYS // SUB
    rows = GROUPS * SUB
    step = pl.program_id(1)
    odd = place_ref[1] == 1

    @pl.when((pl.program_id(0) == 0) & (step == 0))
    def _():
        if not first:
            key_buf[:, HEAD_SIZE:] = key_extra_in[...]
            value_buf[:, HEAD_SIZE:] = value_extra_in[...]
            query_back_ref[...] = query_back_in[...]
            value_back_ref[...] = value_back_in[...]
            return
        first_block = place_ref[0] * (tokens // BLOCK)
        reach = WINDOW // BLOCK
        lane = lax.broadcasted_iota(jnp.int32, (BLOCK, LANES), 1)
        for key_block in range(keys // BLOCK):
            extra = jnp.where(lane == OFFSET_LANE, 1.0, 0.0)
            exists = first_block + (key_block - reach) >= 0
            for block in range(tokens // BLOCK):
                offset = reach + block - key_block
                if 0 <= offset <= reach:
                    hit = (mask_ref[offset, first_block + block] == 1) & exists
                    term = jnp.where(hit, 0.0, FORBIDDEN)
                else:
                    term = FORBIDDEN
                extra = jnp.where(lane == block, term, extra)
            key_buf[key_block * BLOCK : (key_block + 1) * BLOCK, HEAD_SIZE:] = extra.astype(jnp.bfloat16)
        low_far = jnp.where(odd, low_odd_ref[...], low_even_ref[...])
        low = jnp.concatenate([low_far, low_one_ref[...], low_own_ref[...]], axis=1)
        low = jnp.concatenate(
            [
                low.astype(jnp.float32),
                jnp.ones((2, keys), jnp.float32),
                jnp.zeros((LANES - RANK - 2, keys), jnp.float32),
            ],
            axis=0,
        )
        value_buf[:, HEAD_SIZE:] = jnp.transpose(low).astype(jnp.bfloat16)
        key_extra_ref[...] = key_buf[:, HEAD_SIZE:]
        value_extra_ref[...] = value_buf[:, HEAD_SIZE:]
        query_back_ref[...] = jnp.zeros_like(query_back_ref)
        value_back_ref[...] = jnp.zeros_like(value_back_ref)

    @pl.when(step == 0)
    def _():
        key_buf[0:tokens, :HEAD_SIZE] = jnp.where(odd, key_odd_ref[...], key_even_ref[...])
        key_buf[tokens : 2 * tokens, :HEAD_SIZE] = key_one_ref[...]
        key_buf[2 * tokens :, :HEAD_SIZE] = key_own_ref[...]
        value_buf[0:tokens, :HEAD_SIZE] = jnp.where(odd, value_odd_ref[...], value_even_ref[...])
        value_buf[tokens : 2 * tokens, :HEAD_SIZE] = value_one_ref[...]
        value_buf[2 * tokens :, :HEAD_SIZE] = value_own_ref[...]
        up_query_ref[...] = jnp.zeros_like(up_query_ref)
        up_value_ref[...] = jnp.zeros_like(up_value_ref)

    query_up = query_up_ref[...]
    value_up = jnp.concatenate(
        [value_up_ref[...], jnp.zeros((LANES - RANK, HEAD_SIZE), jnp.bfloat16)], axis=0
    )
    lane = lax.broadcasted_iota(jnp.int32, (rows, LANES), 1)
    row = lax.broadcasted_iota(jnp.int32, (rows, LANES), 0) % SUB
    start = pl.multiple_of(step * SUB, SUB)
    window = pl.ds(start, KEYS)
    cosines = cos_ref[...]
    sines = sin_ref[...]

    def own(head):
        return slice(head * SUB, (head + 1) * SUB)

    def head_cols(head):
        return slice(head * HEAD_SIZE, (head + 1) * HEAD_SIZE)

    def near(tile):
        return pl.ds(pl.multiple_of(start + tile * SUB, SUB), SUB)

    def cols(tile):
        return slice(tile * SUB, (tile + 1) * SUB)

    def limit(tile, part):
        if 0 < tile < step_tiles - 1:
            return part
        halves = []
        for block in range(SUB // BLOCK):
            inside = lane > row % BLOCK if tile == 0 else lane <= row % BLOCK
            inside = inside | (row // BLOCK != block)
            halves.append(
                jnp.where(inside, part[:, block * BLOCK : (block + 1) * BLOCK], FORBIDDEN)
            )
        return jnp.concatenate(halves, axis=1)

    reach_of_key = jnp.max(
        jnp.abs(key_buf[window, :HEAD_SIZE].astype(jnp.float32)), axis=0, keepdims=True
    )
    adapted = query_ref[...].astype(jnp.float32) + mm(query_low_ref[...], query_up)
    turned = []
    for head in range(GROUPS):
        part = adapted[:, head_cols(head)]
        turned.append(part * cosines + swap_halves(part) * sines)
    queries = jnp.concatenate(turned, axis=0) * (SCORE_SCALE * LOG2_E)
    bound = jnp.sum(jnp.abs(queries) * reach_of_key, axis=1, keepdims=True)
    chosen = (lane == row // BLOCK + step * (SUB // BLOCK)).astype(jnp.float32)
    query_buf[:, :HEAD_SIZE] = queries.astype(jnp.bfloat16)
    query_buf[:, HEAD_SIZE:] = jnp.where(lane == OFFSET_LANE, -bound, chosen).astype(jnp.bfloat16)
    gradient = jnp.concatenate([gradient_ref[:, head_cols(head)] for head in range(GROUPS)], axis=0)

    def forward():
        for tile in range(step_tiles):
            scores = limit(tile, mm(query_buf[...], key_buf[near(tile), :], BOTH_MINOR))
            weight_buf[:, cols(tile)] = jnp.exp2(scores).astype(jnp.bfloat16)
        product_buf[...] = mm(weight_buf[...], value_buf[window, :])

    forward()
    ones = slice(HEAD_SIZE + ONES_LANE, HEAD_SIZE + ONES_LANE + 1)

    @pl.when(jnp.min(product_buf[:, ones]) < 1e-18)
    def _():
        extra = query_buf[:, HEAD_SIZE:].astype(jnp.float32)
        query_buf[:, HEAD_SIZE:] = jnp.where(lane == OFFSET_LANE, 0.0, extra).astype(jnp.bfloat16)
        highest = jnp.full((rows, 1), FORBIDDEN, jnp.float32)
        for tile in range(step_tiles):
            part = limit(tile, mm(query_buf[...], key_buf[near(tile), :], BOTH_MINOR))
            highest = jnp.maximum(highest, jnp.max(part, axis=1, keepdims=True))
        query_buf[:, HEAD_SIZE:] = jnp.where(lane == OFFSET_LANE, -highest, extra).astype(jnp.bfloat16)
        forward()

    gradient_low = mm(gradient, value_up, BOTH_MINOR)
    inverse = 1.0 / product_buf[:, ones]
    low_part = (product_buf[:, HEAD_SIZE:] * inverse).astype(jnp.bfloat16)
    outputs = product_buf[:, :HEAD_SIZE] * inverse + mm(low_part, value_up)
    outputs = outputs.astype(jnp.bfloat16)
    for head in range(GROUPS):
        out_ref[:, head_cols(head)] = outputs[own(head), :]
    delta = jnp.sum(
        outputs.astype(jnp.float32) * gradient.astype(jnp.float32), axis=1, keepdims=True
    )
    delta_high = delta.astype(jnp.bfloat16).astype(jnp.float32)
    extra = jnp.where(lane == ONES_LANE, -delta_high, gradient_low)
    extra = jnp.where(lane == ONES_LANE + 1, delta_high - delta, extra)
    gradient_buf[:, :HEAD_SIZE] = gradient
    gradient_buf[:, HEAD_SIZE:] = extra.astype(jnp.bfloat16)
    up_value_ref[...] += mm(low_part, gradient, BOTH_MAJOR)[:RANK, :]
    spread = jnp.transpose(gradient_low * inverse)[:RANK, :].astype(jnp.bfloat16)

    for tile in range(step_tiles):
        grad_weights = mm(gradient_buf[...], value_buf[near(tile), :], BOTH_MINOR)
        weights = weight_buf[:, cols(tile)]
        score_buf[:, cols(tile)] = weights * grad_weights.astype(jnp.bfloat16)
        value_back_ref[step + tile] += mm(spread, weights)

    sums = mm(score_buf[...], key_buf[window, :HEAD_SIZE]) * (inverse * SCORE_SCALE)
    turned = []
    for head in range(GROUPS):
        part = sums[own(head), :]
        turned.append(part * cosines - swap_halves(part) * sines)
    query_grad = jnp.concatenate(turned, axis=1).astype(jnp.bfloat16)
    up_query_ref[...] += mm(query_low_t_ref[...], query_grad)
    query_back_ref[step] += mm(query_up, query_grad, BOTH_MINOR)


def attention_chunk(first, last, place, mask, query_base, gradient, received, shared, carried):
    count = last - first
    tokens = query_base.shape[0]
    keys = 3 * tokens
    steps = tokens // SUB
    wide = pl.BlockSpec((SUB, GROUP_WIDTH), lambda i, j, *s: (j, first + i))
    near = pl.BlockSpec((tokens, HEAD_SIZE), lambda i, j, *s: (0, i))
    far = pl.BlockSpec((tokens, HEAD_SIZE), lambda i, j, *s: (0, count + i))
    table = pl.BlockSpec((SUB, HEAD_SIZE), lambda i, j, *s: (j, 0))

    def whole(*shape):
        return pl.BlockSpec(shape, lambda i, j, *s: (0,) * len(shape))

    in_specs = [
        wide,
        wide,
        *([near, far] * 4),
        pl.BlockSpec((RANK, GROUP_WIDTH), lambda i, j, *s: (0, first + i)),
        pl.BlockSpec((RANK, HEAD_SIZE), lambda i, j, *s: (0, first + i)),
        pl.BlockSpec((SUB, RANK), lambda i, j, *s: (j, 0)),
        pl.BlockSpec((RANK, SUB), lambda i, j, *s: (0, j)),
        table,
        table,
    ]
    arguments = [query_base, gradient]
    for array in received:
        arguments += [array, array]
    arguments += shared
    out_specs = [
        wide,
        pl.BlockSpec((RANK, GROUP_WIDTH), lambda i, j, *s: (0, i)),
        pl.BlockSpec((RANK, HEAD_SIZE), lambda i, j, *s: (0, i)),
        whole(steps, RANK, SUB),
        whole(keys // SUB, RANK, SUB),
    ]
    out_shape = [
        jax.ShapeDtypeStruct(query_base.shape, jnp.bfloat16),
        jax.ShapeDtypeStruct((RANK, count * GROUP_WIDTH), jnp.float32),
        jax.ShapeDtypeStruct((RANK, count * HEAD_SIZE), jnp.float32),
        jax.ShapeDtypeStruct((steps, RANK, SUB), jnp.float32),
        jax.ShapeDtypeStruct((keys // SUB, RANK, SUB), jnp.float32),
    ]
    aliases = {}
    if carried is None:
        scalars = (place, mask)
        in_specs += [pl.BlockSpec((RANK, tokens), lambda i, j, *s: (tokens // RANK, 0))] * 4
        arguments += received
        out_specs += [whole(keys, LANES)] * 2
        out_shape += [jax.ShapeDtypeStruct((keys, LANES), jnp.bfloat16)] * 2
    else:
        scalars = (place,)
        in_specs += [
            whole(keys, LANES),
            whole(keys, LANES),
            pl.BlockSpec(memory_space=pl.ANY),
            whole(steps, RANK, SUB),
            whole(keys // SUB, RANK, SUB),
        ]
        arguments += carried
        aliases = {len(scalars) + len(arguments) - 3: 0}
    rows = GROUPS * SUB
    wide_buf = HEAD_SIZE + LANES
    return pl.pallas_call(
        functools.partial(attention_kernel, carried is None),
        grid_spec=pltpu.PrefetchScalarGridSpec(
            num_scalar_prefetch=len(scalars),
            grid=(count, steps),
            in_specs=in_specs,
            out_specs=out_specs,
            scratch_shapes=[
                pltpu.VMEM((keys, wide_buf), jnp.bfloat16),
                pltpu.VMEM((keys, wide_buf), jnp.bfloat16),
                pltpu.VMEM((rows, wide_buf), jnp.bfloat16),
                pltpu.VMEM((rows, wide_buf), jnp.bfloat16),
                pltpu.VMEM((rows, KEYS), jnp.bfloat16),
                pltpu.VMEM((rows, KEYS), jnp.bfloat16),
                pltpu.VMEM((rows, wide_buf), jnp.float32),
            ],
        ),
        out_shape=out_shape,
        input_output_aliases=aliases,
        compiler_params=pltpu.CompilerParams(vmem_limit_bytes=32 * 2**20),
    )(*scalars, *arguments)


def head_sum(x):
    if lax.axis_size("head") == 2:
        return x + lax.ppermute(x, "head", [(0, 1), (1, 0)])
    return lax.psum(x, "head")


def group_exchange(x, groups):
    return lax.all_to_all(x, "ctx", 0, 0, axis_index_groups=groups)


def ctx_sum(x):
    devices = lax.axis_size("ctx")
    near = 4 if devices % 4 == 0 else 1
    far = devices // near
    near_groups = [[i * near + j for j in range(near)] for i in range(far)]
    far_groups = [[i * near + j for i in range(far)] for j in range(near)]
    columns = x.shape[1]
    piece = -(-columns // (near * LANES)) * LANES
    x = jnp.pad(x, ((0, 0), (0, near * piece - columns)))
    x = jnp.stack([x[:, i * piece : (i + 1) * piece] for i in range(near)])
    mine = jnp.sum(group_exchange(x, near_groups).astype(jnp.float32), axis=0).astype(jnp.bfloat16)
    mine = group_exchange(jnp.broadcast_to(mine[None], (far, RANK, piece)), far_groups)
    mine = jnp.sum(mine.astype(jnp.float32), axis=0).astype(jnp.bfloat16)
    x = group_exchange(jnp.broadcast_to(mine[None], (near, RANK, piece)), near_groups)
    return jnp.concatenate([x[i] for i in range(near)], axis=1)[:, :columns].astype(jnp.float32)


def after(value, *others):
    return lax.optimization_barrier((value, *others))[0]


def per_device(
    hidden_states,
    query_base,
    key_base,
    frozen_value_rows,
    query_down,
    query_up,
    value_down,
    value_up_weight,
    positions,
    block_mask,
    output_gradient,
):
    tokens = hidden_states.shape[0]
    devices = lax.axis_size("ctx")
    device_index = lax.axis_index("ctx")
    kv_heads = key_base.shape[1] // HEAD_SIZE
    forward_one = [(i, i + 1) for i in range(devices - 1)]
    even_two = [(i, i + 2) for i in range(0, devices - 2, 2)]
    even_one = [(i, i + 1) for i in range(0, devices - 1, 2)]

    both_down = jnp.concatenate([query_down, value_down], axis=1)
    low = head_sum(mm(both_down, hidden_states, (((0,), (1,)), ((), ())))).astype(jnp.bfloat16)
    query_low_t = low[:RANK]
    value_low_t = low[RANK:]

    half = np.arange(HEAD_SIZE // 2, dtype=np.float64)
    frequency = (ROPE_BASE ** (-2.0 * half / HEAD_SIZE)).astype(np.float32)[:, None]
    cosines, sines, *packed = pl.pallas_call(
        functools.partial(prologue_kernel, CHUNKS),
        out_shape=[
            jax.ShapeDtypeStruct((tokens, HEAD_SIZE), jnp.float32),
            jax.ShapeDtypeStruct((tokens, HEAD_SIZE), jnp.float32),
            *(
                jax.ShapeDtypeStruct(
                    (tokens + (RANK if first == 0 else 0), 2 * (last - first) * HEAD_SIZE),
                    jnp.bfloat16,
                )
                for first, last in CHUNKS
            ),
        ],
        compiler_params=pltpu.CompilerParams(vmem_limit_bytes=50 * 2**20),
    )(positions[None, :], jnp.asarray(frequency), key_base, frozen_value_rows)
    packed[0] = lax.dynamic_update_slice(packed[0], value_low_t, (tokens, 0))

    place = jnp.stack([device_index, device_index % 2]).astype(jnp.int32)
    shared = [query_up, value_up_weight, query_low_t.T, query_low_t, cosines, sines]

    ones, evens = [], []
    for chunk, own in enumerate(packed):
        if chunk > 0:
            own = after(own, ones[chunk - 1], evens[chunk - 1])
        ones.append(lax.ppermute(own, "ctx", forward_one))
        evens.append(lax.ppermute(own, "ctx", even_two))

    carried = None
    up_queries, up_values = [], []
    for chunk, (first, last) in enumerate(CHUNKS):
        one = ones[chunk]
        if carried is not None:
            one = after(one, carried[3])
        odd = lax.ppermute(one, "ctx", even_one)
        received = [packed[chunk], one, evens[chunk], odd]
        attention_out, up_query, up_value, query_back, value_back, *tables = attention_chunk(
            first,
            last,
            place,
            block_mask.T,
            query_base,
            output_gradient,
            received,
            shared,
            carried,
        )
        if carried is None:
            extras = tables
        carried = [*extras, attention_out, query_back, value_back]
        up_queries.append(up_query)
        up_values.append(up_value)

    steps = tokens // SUB
    back_one = lax.ppermute(value_back[steps : 2 * steps], "ctx", [(i + 1, i) for i in range(devices - 1)])
    back_two = lax.ppermute(value_back[:steps], "ctx", [(i + 2, i) for i in range(devices - 2)])
    value_back = value_back[2 * steps :] + back_one + back_two
    back = head_sum(jnp.concatenate([query_back, value_back], axis=1))
    back = jnp.concatenate([back[step] for step in range(steps)], axis=1).astype(jnp.bfloat16)
    down = mm(back, hidden_states)
    features = down.shape[1]
    partial = jnp.concatenate([down[:RANK], down[RANK:], *up_queries, *up_values], axis=1)
    summed = ctx_sum(partial.astype(jnp.bfloat16)) * ((devices * tokens) ** (-0.5))
    query_columns = kv_heads * GROUP_WIDTH
    up_first = 2 * features
    return (
        attention_out,
        summed[:, :features].T,
        summed[:, up_first : up_first + query_columns],
        summed[:, features:up_first].T,
        summed[:, up_first + query_columns :],
    )


def solution(mesh):
    placed = (
        P("ctx", "head"),
        P("ctx", "head"),
        P("ctx", "head"),
        P("ctx", "head"),
        P("head", None),
        P(None, "head"),
        P("head", None),
        P(None, "head"),
        P("ctx"),
        P(),
        P("ctx", "head"),
    )
    return jax.shard_map(
        per_device,
        mesh=mesh,
        in_specs=placed,
        out_specs=(
            P("ctx", "head"),
            P("head", None),
            P(None, "head"),
            P("head", None),
            P(None, "head"),
        ),
        check_vma=False,
    )
```

time: 182 us -> 202 us (1.11)
  Pallas kernels: 78.7 us -> 95.4 us
  starting transfers between devices: 43 us -> 29.4 us
  waiting for transfers between devices: 10.6 us -> 20 us
  local copies, waits for them, and re-layouts: 13.9 us -> 20 us
    pallas_call x4 -> x3, Pallas kernels: 75.2 us -> 92 us  [attention_chunk(): pl.pallas_call(functools.partial(attention_kernel, carried is None), grid...]
    ppermute x4 -> x3, starting transfers between devices: 14.1 us -> 4.77 us  [per_device(): odd = lax.ppermute(one, 'ctx', even_one)]
    ppermute x4 -> x3, waiting for transfers between devices: 0.01 us -> 9.31 us  [per_device(): evens.append(lax.ppermute(own, 'ctx', even_two))]
    unnamed x44 -> x53, local copies, waits for them, and re-layouts: 9.63 us -> 15.8 us
    ppermute x4 -> x3, starting transfers between devices: 16.5 us -> 13.5 us  [per_device(): evens.append(lax.ppermute(own, 'ctx', even_two))]
    ppermute x4 -> x3, starting transfers between devices: 6.21 us -> 5.01 us  [per_device(): ones.append(lax.ppermute(own, 'ctx', forward_one))]
    all_to_all x2 -> x3, blocking collectives: 30.8 us -> 31.8 us  [group_exchange(): return lax.all_to_all(x, 'ctx', 0, 0, axis_index_groups=groups)]
  transfers between devices with their start and end apart: 16 -> 13, of which waited for: 4 -> 5; matrix products, arithmetic and copies ran while one was open for 1% -> 1% of each run, Pallas kernels for 33% -> 31%
where the time goes in v3:
time: 202 us; the launch traced here: 201 us
  Pallas kernels  95.4 us (47%)
  blocking collectives  31.8 us (16%)
  starting transfers between devices  29.4 us (15%)
  local copies, waits for them, and re-layouts  20 us (10%)
  waiting for transfers between devices  20 us (10%)
  matrix products  2.4 us (1%)
    pallas_call x3, Pallas kernels, attention_chunk(): pl.pallas_call(functools.partial(attention_kernel, carried is None), grid...  92 us
    all_to_all x3, blocking collectives, group_exchange(): return lax.all_to_all(x, 'ctx', 0, 0, axis_index_groups=groups)  31.8 us
    unnamed x53, local copies, waits for them, and re-layouts  15.8 us
    ppermute x3, starting transfers between devices, per_device(): evens.append(lax.ppermute(own, 'ctx', even_two))  13.5 us
    ppermute x3, waiting for transfers between devices, per_device(): evens.append(lax.ppermute(own, 'ctx', even_two))  9.31 us
    ppermute x3, starting transfers between devices, per_device(): ones.append(lax.ppermute(own, 'ctx', forward_one))  5.01 us
    ppermute x3, starting transfers between devices, per_device(): odd = lax.ppermute(one, 'ctx', even_one)  4.77 us
    ppermute x1, waiting for transfers between devices, per_device(): lax.ppermute(value_back[:steps], 'ctx', [(i + 2, i) for i in range(device...  4.61 us
  transfers between devices with their start and end apart: 13, of which 5 were waited for; matrix products, arithmetic and copies ran while one was open for 1% of the time, Pallas kernels for 31%

profile of v3, /device:TPU:0, one launch (start us, length us, event | category | flops | bytes accessed | tf_op | source)
XLA Modules:
  0.0 201.1 jit_solution(8321042315671963172)
XLA Ops:
  0.7 1.7 copy-done
  2.4 1.8 fusion
  4.2 3.0 %collective-permute-start = (f32[32,512]{1,0:T(8,128)S(1)}, f32[32,512]{1,0:T(8,128)S(1)}, u32[]{:S(2)}, u32[]{:S(2)}) collective-permute-start(f32[32,512]{1,0:T(8,128)S(1)} %fusion), channel_id=1, source_target_pairs={{0,1},{1,0},{2,3},{3,2},{4,5},{5,4},{6,7},{7,6},{8,9},{9,8},{10,11... | collective-permute-start | bytes 196616 | tf_op jit(solution)/shard_map/ppermute | solution.py:347
  7.2 3.4 %shard_map.155 = (f32[512,128]{1,0:T(8,128)S(1)}, f32[512,128]{1,0:T(8,128)S(1)}, bf16[528,512]{1,0:T(8,128)(2,1)S(1)}, bf16[512,768]{1,0:T(8,128)(2,1)}, bf16[512,768]{1,0:T(8,128)(2,1)S(1)}) custom-call(s32[1,512]{1,0:T(1,128)S(1)} %bitcast.33, f32[64,1]{1,0:T(8,128)S(1)} %copy-done.21, bf16[512,1024]{1,0:T(8,128)(2,1)S(1)} %copy-done.14, ...), custom_call_target="tpu_custom_call" | custom-call | tf_op jit(solution)/shard_map/pallas_call | solution.py:404
  12.8 1.5 collective-permute-start.1
  14.3 3.9 %collective-permute-start.2 = (bf16[528,512]{1,0:T(8,128)(2,1)S(1)}, bf16[528,512]{1,0:T(8,128)(2,1)S(1)}, u32[]{:S(2)}, u32[]{:S(2)}) collective-permute-start(bf16[528,512]{1,0:T(8,128)(2,1)S(1)} %get-tuple-element.78.refs_3_.refs_4_.refs_17_), channel_id=1, source_target_pairs={{0,4},{4,8},{8,12},{12,16},{16,20},{20,24},{24,28},{1,5},{5,9},{9,... | collective-permute-start | bytes 1622024 | tf_op jit(solution)/shard_map/ppermute | solution.py:429
  19.0 9.3 %collective-permute-done.2.refs_7_.refs_8_.refs_19_ = bf16[528,512]{1,0:T(8,128)(2,1)S(1)} collective-permute-done((bf16[528,512]{1,0:T(8,128)(2,1)S(1)}, bf16[528,512]{1,0:T(8,128)(2,1)S(1)}, u32[]{:S(2)}, u32[]{:S(2)}) %collective-permute-start.2) | collective-permute-done | bytes 540704 | tf_op jit(solution)/shard_map/ppermute | solution.py:429
  29.1 2.2 %collective-permute-start.3 = (bf16[512,768]{1,0:T(8,128)(2,1)}, bf16[512,768]{1,0:T(8,128)(2,1)}, u32[]{:S(2)}, u32[]{:S(2)}) collective-permute-start(bf16[512,768]{1,0:T(8,128)(2,1)} %get-tuple-element.34.refs_2_.refs_3_), channel_id=1, source_target_pairs={{0,2},{2,4},{4,6},{6,8},{8,10},{10,12},{12,14},{14,16},{16,18},{18... | collective-permute-start | bytes 2359304 | tf_op jit(solution)/shard_map/ppermute | solution.py:428
  31.3 5.0 %collective-permute-start.4 = (bf16[512,768]{1,0:T(8,128)(2,1)}, bf16[512,768]{1,0:T(8,128)(2,1)}, u32[]{:S(2)}, u32[]{:S(2)}) collective-permute-start(bf16[512,768]{1,0:T(8,128)(2,1)} %get-tuple-element.34.refs_2_.refs_3_), channel_id=1, source_target_pairs={{0,4},{4,8},{8,12},{12,16},{16,20},{20,24},{24,28},{1,5},{5,9},{9,... | collective-permute-start | bytes 2359304 | tf_op jit(solution)/shard_map/ppermute | solution.py:429
  36.3 2.1 %collective-permute-start.6 = (bf16[528,512]{1,0:T(8,128)(2,1)S(1)}, bf16[528,512]{1,0:T(8,128)(2,1)}, u32[]{:S(2)}, u32[]{:S(2)}) collective-permute-start(bf16[528,512]{1,0:T(8,128)(2,1)S(1)} %collective-permute-done.1.refs_5_.refs_6_.refs_18_), channel_id=1, source_target_pairs={{0,2},{4,6},{8,10},{12,14},{16,18},{20,22},{24,26},{28,30},{1,3},{... | collective-permute-start | bytes 1622024 | tf_op jit(solution)/shard_map/ppermute | solution.py:437
  39.1 1.5 copy.22.refs_13_.refs_12_
  40.6 1.6 copy-done.1
  42.2 1.6 copy-done.3
  43.7 1.0 copy-done.5
  44.8 1.0 copy-done.7
  45.8 0.9 copy-done.11
  46.8 0.9 copy-done.12
  51.4 23.8 %shard_map.156 = (bf16[512,2048]{1,0:T(8,128)(2,1)}, f32[16,512]{1,0:T(8,128)S(1)}, f32[16,256]{1,0:T(8,128)S(1)}, f32[2,16,256]{2,1,0:T(8,128)S(1)}, f32[6,16,2...) custom-call(s32[2]{0:T(128)S(1)} %copy-done.23, s32[9,64]{1,0:T(8,128)S(1)} %bitcast.32, ...), custom_call_target="tpu_custom_call" | custom-call | tf_op jit(solution)/shard_map/pallas_call | solution.py:322
  75.2 1.3 collective-permute-start.7
  76.6 1.3 collective-permute-start.5
  78.0 4.6 %collective-permute-start.8 = (bf16[512,768]{1,0:T(8,128)(2,1)S(1)}, bf16[512,768]{1,0:T(8,128)(2,1)S(1)}, u32[]{:S(2)}, u32[]{:S(2)}) collective-permute-start(bf16[512,768]{1,0:T(8,128)(2,1)S(1)} %copy-done.9), channel_id=1, source_target_pairs={{0,4},{4,8},{8,12},{12,16},{16,20},{20,24},{24,28},{1,5},{5,9},{9,... | collective-permute-start | bytes 2359304 | tf_op jit(solution)/shard_map/ppermute | solution.py:429
  82.6 34.5 %shard_map.157 = (bf16[512,2048]{1,0:T(8,128)(2,1)}, f32[16,768]{1,0:T(8,128)S(1)}, f32[16,384]{1,0:T(8,128)S(1)}, f32[2,16,256]{2,1,0:T(8,128)S(1)}, f32[6,16,256]{2,1,0:T(8,128)S(1)}) custom-call(s32[2]{0:T(128)S(1)} %copy-done.24, bf16[512,2048]{1,0:T(8,128)(2,1)S(1)} %copy-done.2, ...), custom_call_target="tpu_custom_call", output_to_operand_aliasing={{0}: (19, {})} | custom-call | tf_op jit(solution)/shard_map/pallas_call | solution.py:322
  117.1 1.3 collective-permute-start.9
  118.5 1.8 collective-permute-done.9.refs_8_.refs_9_
  120.3 33.7 %shard_map.158 = (bf16[512,2048]{1,0:T(8,128)(2,1)}, f32[16,768]{1,0:T(8,128)S(1)}, f32[16,384]{1,0:T(8,128)S(1)}, f32[2,16,256]{2,1,0:T(8,128)S(1)}, f32[6,16,256]{2,1,0:T(8,128)S(1)}) custom-call(s32[2]{0:T(128)S(1)} %copy-done.24, bf16[512,2048]{1,0:T(8,128)(2,1)S(1)} %copy-done.2, ...), custom_call_target="tpu_custom_call", output_to_operand_aliasing={{0}: (19, {})} | custom-call | tf_op jit(solution)/shard_map/pallas_call | solution.py:322
  154.1 1.3 collective-permute-start.10
  155.4 1.3 collective-permute-start.11
  157.2 4.6 %collective-permute-done.11 = f32[2,16,256]{2,1,0:T(8,128)S(1)} collective-permute-done((f32[2,16,256]{2,1,0:T(8,128)S(1)}, f32[2,16,256]{2,1,0:T(8,128)S(1)}, u32[]{:S(2)}, u32[]{:S(2)}) %collective-permute-start.11) | collective-permute-done | bytes 32800 | tf_op jit(solution)/shard_map/ppermute | solution.py:458
  162.4 3.7 %collective-permute-done.12 = f32[2,32,256]{2,1,0:T(8,128)S(1)} collective-permute-done((f32[2,32,256]{2,1,0:T(8,128)S(1)}, f32[2,32,256]{2,1,0:T(8,128)S(1)}, u32[]{:S(2)}, u32[]{:S(2)}) %collective-permute-start.12) | collective-permute-done | bytes 65568 | tf_op jit(solution)/shard_map/ppermute | solution.py:347
  167.0 10.2 %all_to_all.15 = bf16[4,16,2176]{2,1,0:T(8,128)(2,1)S(1)} all-to-all(bf16[4,16,2176]{2,1,0:T(8,128)(2,1)S(1)} %pad_maximum_fusion), channel_id=1, replica_groups={{0,2,4,6},{8,10,12,14},{16,18,20,22},{24,26,28,30},{1,3,5,7},{9,11,13,1..., dimensions={0} | all-to-all | bytes 557056 | tf_op jit(solution)/shard_map/all_to_all | solution.py:352
  177.3 13.0 %all_to_all.16 = bf16[4,16,2176]{2,1,0:T(8,128)(2,1)S(1)} all-to-all(bf16[4,16,2176]{2,1,0:T(8,128)(2,1)S(1)} %broadcast_in_dim.7), channel_id=1, replica_groups={{0,8,16,24},{2,10,18,26},{4,12,20,28},{6,14,22,30},{1,9,17,25},{3,11,19..., dimensions={0} | all-to-all | bytes 557056 | tf_op jit(solution)/shard_map/all_to_all | solution.py:352
  190.4 8.6 %all_to_all.17 = bf16[4,16,2176]{2,1,0:T(8,128)(2,1)S(1)} all-to-all(bf16[4,16,2176]{2,1,0:T(8,128)(2,1)S(1)} %broadcast_in_dim.8), channel_id=1, replica_groups={{0,2,4,6},{8,10,12,14},{16,18,20,22},{24,26,28,30},{1,3,5,7},{9,11,13,1..., dimensions={0} | all-to-all | bytes 557056 | tf_op jit(solution)/shard_map/all_to_all | solution.py:352
  (84 shorter events, 12.3 us)
Async XLA Ops:
  0.6 1.8 copy-start
  0.6 6.6 %copy-start.21 = (f32[64,1]{1,0:T(8,128)S(1)}, f32[64,1]{1,0:T(8,128)}, u32[]{:S(2)}) copy-start(f32[64,1]{1,0:T(8,128)} %constant.31.clone.frequency_ref) | copy-start | bytes 772
  0.7 6.5 %copy-start.25 = (s32[512]{0:T(512)S(1)}, s32[512]{0:T(512)}, u32[]{:S(2)}) copy-start(s32[512]{0:T(512)} %param.20) | copy-start | bytes 6148
  0.7 6.5 %copy-start.14 = (bf16[512,1024]{1,0:T(8,128)(2,1)S(1)}, bf16[512,1024]{1,0:T(8,128)(2,1)}, u32[]{:S(2)}) copy-start(bf16[512,1024]{1,0:T(8,128)(2,1)} %key_ref.1) | copy-start | bytes 3145732
  4.2 8.0 %collective-permute-start = (f32[32,512]{1,0:T(8,128)S(1)}, f32[32,512]{1,0:T(8,128)S(1)}, u32[]{:S(2)}, u32[]{:S(2)}) collective-permute-start(f32[32,512]{1,0:T(8,128)S(1)} %fusion), channel_id=1, source_target_pairs={{0,1},{1,0},{2,3},{3,2},{4,5},{5,4},{6,7},{7,6},{8,9},{9,8},{10,11... | collective-permute-start | bytes 196616 | tf_op jit(solution)/shard_map/ppermute | solution.py:347
  10.6 0.9 copy-start.8
  12.8 6.2 %collective-permute-start.1 = (bf16[528,512]{1,0:T(8,128)(2,1)S(1)}, bf16[528,512]{1,0:T(8,128)(2,1)S(1)}, u32[]{:S(2)}, u32[]{:S(2)}) collective-permute-start(bf16[528,512]{1,0:T(8,128)(2,1)S(1)} %get-tuple-element.78.refs_3_.refs_4_.refs_17_), channel_id=1, source_target_pairs={{0,2},{2,4},{4,6},{6,8},{8,10},{10,12},{12,14},{14,16},{16,18},{18... | collective-permute-start | bytes 1622024 | tf_op jit(solution)/shard_map/ppermute | solution.py:428
  14.3 14.0 %collective-permute-start.2 = (bf16[528,512]{1,0:T(8,128)(2,1)S(1)}, bf16[528,512]{1,0:T(8,128)(2,1)S(1)}, u32[]{:S(2)}, u32[]{:S(2)}) collective-permute-start(bf16[528,512]{1,0:T(8,128)(2,1)S(1)} %get-tuple-element.78.refs_3_.refs_4_.refs_17_), channel_id=1, source_target_pairs={{0,4},{4,8},{8,12},{12,16},{16,20},{20,24},{24,28},{1,5},{5,9},{9,... | collective-permute-start | bytes 1622024 | tf_op jit(solution)/shard_map/ppermute | solution.py:429
  29.1 46.1 %collective-permute-start.3 = (bf16[512,768]{1,0:T(8,128)(2,1)}, bf16[512,768]{1,0:T(8,128)(2,1)}, u32[]{:S(2)}, u32[]{:S(2)}) collective-permute-start(bf16[512,768]{1,0:T(8,128)(2,1)} %get-tuple-element.34.refs_2_.refs_3_), channel_id=1, source_target_pairs={{0,2},{2,4},{4,6},{6,8},{8,10},{10,12},{12,14},{14,16},{16,18},{18... | collective-permute-start | bytes 2359304 | tf_op jit(solution)/shard_map/ppermute | solution.py:428
  31.3 45.3 %collective-permute-start.4 = (bf16[512,768]{1,0:T(8,128)(2,1)}, bf16[512,768]{1,0:T(8,128)(2,1)}, u32[]{:S(2)}, u32[]{:S(2)}) collective-permute-start(bf16[512,768]{1,0:T(8,128)(2,1)} %get-tuple-element.34.refs_2_.refs_3_), channel_id=1, source_target_pairs={{0,4},{4,8},{8,12},{12,16},{16,20},{20,24},{24,28},{1,5},{5,9},{9,... | collective-permute-start | bytes 2359304 | tf_op jit(solution)/shard_map/ppermute | solution.py:429
  36.3 4.2 %collective-permute-start.6 = (bf16[528,512]{1,0:T(8,128)(2,1)S(1)}, bf16[528,512]{1,0:T(8,128)(2,1)}, u32[]{:S(2)}, u32[]{:S(2)}) collective-permute-start(bf16[528,512]{1,0:T(8,128)(2,1)S(1)} %collective-permute-done.1.refs_5_.refs_6_.refs_18_), channel_id=1, source_target_pairs={{0,2},{4,6},{8,10},{12,14},{16,18},{20,22},{24,26},{28,30},{1,3},{... | collective-permute-start | bytes 1622024 | tf_op jit(solution)/shard_map/ppermute | solution.py:437
  40.6 1.6 copy-start.1
  42.2 1.6 copy-start.3
  43.7 1.0 copy-start.5
  44.8 1.0 copy-start.7
  45.8 0.9 copy-start.11
  46.8 0.9 copy-start.12
  47.7 0.8 copy-start.15
  51.4 25.2 %copy-start.9 = (bf16[512,768]{1,0:T(8,128)(2,1)S(1)}, bf16[512,768]{1,0:T(8,128)(2,1)}, u32[]{:S(2)}) copy-start(bf16[512,768]{1,0:T(8,128)(2,1)} %copy-done.8) | copy-start | bytes 2359300
  51.4 31.2 %copy-start.2 = (bf16[512,2048]{1,0:T(8,128)(2,1)S(1)}, bf16[512,2048]{1,0:T(8,128)(2,1)}, u32[]{:S(2)}) copy-start(bf16[512,2048]{1,0:T(8,128)(2,1)} %refs_0_.3) | copy-start | bytes 6291460
  51.4 31.2 %copy-start.13 = (bf16[512,16]{1,0:T(8,128)(2,1)S(1)}, bf16[512,16]{1,0:T(8,128)(2,1)}, u32[]{:S(2)}) copy-start(bf16[512,16]{1,0:T(8,128)(2,1)} %copy.22.refs_13_.refs_12_) | copy-start | bytes 49156
  51.4 31.2 %copy-start.16 = (bf16[16,2048]{1,0:T(8,128)(2,1)S(1)}, bf16[16,2048]{1,0:T(8,128)(2,1)}, u32[]{:S(2)}) copy-start(bf16[16,2048]{1,0:T(8,128)(2,1)} %refs_10_.3) | copy-start | bytes 196612
  51.4 31.2 %copy-start.18 = (bf16[16,1024]{1,0:T(8,128)(2,1)S(1)}, bf16[16,1024]{1,0:T(8,128)(2,1)}, u32[]{:S(2)}) copy-start(bf16[16,1024]{1,0:T(8,128)(2,1)} %refs_11_.5) | copy-start | bytes 98308
  51.4 31.2 %copy-start.20 = (bf16[16,512]{1,0:T(8,128)(2,1)S(1)}, bf16[16,512]{1,0:T(8,128)(2,1)}, u32[]{:S(2)}) copy-start(bf16[16,512]{1,0:T(8,128)(2,1)} %get-tuple-element.76.refs_14_.refs_13_) | copy-start | bytes 49156
  51.4 31.2 %copy-start.24 = (s32[2]{0:T(128)S(1)}, s32[2]{0:T(128)}, u32[]{:S(2)}) copy-start(s32[2]{0:T(128)} %pad_add_fusion.place_ref) | copy-start | bytes 28
  75.2 7.3 %collective-permute-start.7 = (bf16[512,768]{1,0:T(8,128)(2,1)}, bf16[512,768]{1,0:T(8,128)(2,1)S(1)}, u32[]{:S(2)}, u32[]{:S(2)}) collective-permute-start(bf16[512,768]{1,0:T(8,128)(2,1)} %collective-permute-done.3.refs_4_.refs_5_), channel_id=1, source_target_pairs={{0,2},{4,6},{8,10},{12,14},{16,18},{20,22},{24,26},{28,30},{1,3},{... | collective-permute-start | bytes 2359304 | tf_op jit(solution)/shard_map/ppermute | solution.py:437
  76.6 40.5 %collective-permute-start.5 = (bf16[512,768]{1,0:T(8,128)(2,1)S(1)}, bf16[512,768]{1,0:T(8,128)(2,1)S(1)}, u32[]{:S(2)}, u32[]{:S(2)}) collective-permute-start(bf16[512,768]{1,0:T(8,128)(2,1)S(1)} %copy-done.9), channel_id=1, source_target_pairs={{0,2},{2,4},{4,6},{6,8},{8,10},{10,12},{12,14},{14,16},{16,18},{18... | collective-permute-start | bytes 2359304 | tf_op jit(solution)/shard_map/ppermute | solution.py:428
  78.0 40.5 %collective-permute-start.8 = (bf16[512,768]{1,0:T(8,128)(2,1)S(1)}, bf16[512,768]{1,0:T(8,128)(2,1)S(1)}, u32[]{:S(2)}, u32[]{:S(2)}) collective-permute-start(bf16[512,768]{1,0:T(8,128)(2,1)S(1)} %copy-done.9), channel_id=1, source_target_pairs={{0,4},{4,8},{8,12},{12,16},{16,20},{20,24},{24,28},{1,5},{5,9},{9,... | collective-permute-start | bytes 2359304 | tf_op jit(solution)/shard_map/ppermute | solution.py:429
  117.1 3.2 %collective-permute-start.9 = (bf16[512,768]{1,0:T(8,128)(2,1)S(1)}, bf16[512,768]{1,0:T(8,128)(2,1)S(1)}, u32[]{:S(2)}, u32[]{:S(2)}) collective-permute-start(bf16[512,768]{1,0:T(8,128)(2,1)S(1)} %collective-permute-done.5.refs_4_.refs_5_), channel_id=1, source_target_pairs={{0,2},{4,6},{8,10},{12,14},{16,18},{20,22},{24,26},{28,30},{1,3},{... | collective-permute-start | bytes 2359304 | tf_op jit(solution)/shard_map/ppermute | solution.py:437
  154.1 3.1 %collective-permute-start.10 = (f32[2,16,256]{2,1,0:T(8,128)S(1)}, f32[2,16,256]{2,1,0:T(8,128)S(1)}, u32[]{:S(2)}, u32[]{:S(2)}) collective-permute-start(f32[2,16,256]{2,1,0:T(8,128)S(1)} %get-tuple-element.70), channel_id=1, source_target_pairs={{2,0},{4,2},{6,4},{8,6},{10,8},{12,10},{14,12},{16,14},{18,16},{20... | collective-permute-start | bytes 98312 | tf_op jit(solution)/shard_map/ppermute | solution.py:457
  155.4 6.4 %collective-permute-start.11 = (f32[2,16,256]{2,1,0:T(8,128)S(1)}, f32[2,16,256]{2,1,0:T(8,128)S(1)}, u32[]{:S(2)}, u32[]{:S(2)}) collective-permute-start(f32[2,16,256]{2,1,0:T(8,128)S(1)} %get-tuple-element.71), channel_id=1, source_target_pairs={{4,0},{6,2},{8,4},{10,6},{12,8},{14,10},{16,12},{18,14},{20,16},{2... | collective-permute-start | bytes 98312 | tf_op jit(solution)/shard_map/ppermute | solution.py:458
  161.8 4.3 %collective-permute-start.12 = (f32[2,32,256]{2,1,0:T(8,128)S(1)}, f32[2,32,256]{2,1,0:T(8,128)S(1)}, u32[]{:S(2)}, u32[]{:S(2)}) collective-permute-start(f32[2,32,256]{2,1,0:T(8,128)S(1)} %pad_maximum_fusion.7), channel_id=1, source_target_pairs={{0,1},{1,0},{2,3},{3,2},{4,5},{5,4},{6,7},{7,6},{8,9},{9,8},{10,11... | collective-permute-start | bytes 196616 | tf_op jit(solution)/shard_map/ppermute | solution.py:347
  (7 other events, 5.2 us)
